TPU v7x, 32 devices: a whole 2x2x4 slice. The times are simulated.
32 devices in a mesh: fsdp: 2 (over x), ctx: 4 (over z), tp: 4 (over y, core).
Axes of the slice: x: 2, y: 2, z: 4, core: 2. Of those that a mesh axis runs over, the one named last changes fastest.
Arguments:
- activations: bfloat16 [2048, 2560], P(('fsdp', 'ctx'), 'tp'), may hold values from -6 to 6
- attn_gain: bfloat16 [2560], P('tp'), may hold values from 0.099609375 to 1.8984375
- query_down: bfloat16 [2560, 768], P('tp', ('fsdp', 'ctx')), may hold values from -0.125 to 0.125
- latent_down: bfloat16 [2560, 288], P('tp', ('fsdp', 'ctx')), may hold values from -0.125 to 0.125
- query_gain: bfloat16 [768], P(('fsdp', 'ctx')), may hold values from 0.099609375 to 1.8984375
- latent_gain: bfloat16 [256], P(('fsdp', 'ctx')), may hold values from 0.099609375 to 1.8984375
- query_up: bfloat16 [768, 3840], P(('fsdp', 'ctx'), 'tp'), may hold values from -0.21875 to 0.21875
- latent_up: bfloat16 [256, 5120], P(('fsdp', 'ctx'), 'tp'), may hold values from -0.375 to 0.375
- attn_output: bfloat16 [2560, 2560], P('tp', ('fsdp', 'ctx')), may hold values from -12 to 12
- ffn_gain: bfloat16 [2560], P('tp'), may hold values from 0.099609375 to 1.8984375
- ffn_gate: bfloat16 [2560, 6400], P(('fsdp', 'ctx'), 'tp'), may hold values from -0.125 to 0.125
- ffn_up: bfloat16 [2560, 6400], P(('fsdp', 'ctx'), 'tp'), may hold values from -0.125 to 0.125
- ffn_down: bfloat16 [6400, 2560], P('tp', ('fsdp', 'ctx')), may hold values from -0.8984375 to 0.8984375
- out_grad: bfloat16 [2048, 2560], P(('fsdp', 'ctx'), 'tp'), may hold values from -6 to 6
Outputs:
- result: bfloat16 [2048, 2560], P(('fsdp', 'ctx'), 'tp')
- input_grad: float32 [2048, 2560], P(('fsdp', 'ctx'), 'tp')
- attn_gain_grad: float32 [2560], P('tp')
- query_down_grad: float32 [2560, 768], P('tp', ('fsdp', 'ctx'))
- latent_down_grad: float32 [2560, 288], P('tp', ('fsdp', 'ctx'))
- query_gain_grad: float32 [768], P(('fsdp', 'ctx'))
- latent_gain_grad: float32 [256], P(('fsdp', 'ctx'))
- query_up_grad: float32 [768, 3840], P(('fsdp', 'ctx'), 'tp')
- latent_up_grad: float32 [256, 5120], P(('fsdp', 'ctx'), 'tp')
- attn_output_grad: float32 [2560, 2560], P('tp', ('fsdp', 'ctx'))
- ffn_gain_grad: float32 [2560], P('tp')
- ffn_gate_grad: float32 [2560, 6400], P(('fsdp', 'ctx'), 'tp')
- ffn_up_grad: float32 [2560, 6400], P(('fsdp', 'ctx'), 'tp')
- ffn_down_grad: float32 [6400, 2560], P('tp', ('fsdp', 'ctx'))
All inputs are finite; a program needn't handle non-finite values.
Results may differ from a plain program's by a relative error of at most 0.02.
Values may be sent and summed in bfloat16 or wider, within the bound.
No kernel may reach another device: no remote copies, remote signals or barrier semaphores. Data moves between devices by JAX's collectives and lax.ppermute only.
A program may use at most 192 MiB of HBM per device.

v0:
```python
import functools
import math

import jax
import jax.numpy as jnp
import numpy as np
from jax import lax
from jax.experimental import pallas as pl
from jax.experimental.pallas import tpu as pltpu
from jax.sharding import PartitionSpec as P

NOPE = 64
ROPE = 32
VDIM = 64
QRANK = 768
KVRANK = 256
LANES = 128
SUBLANES = 16

RESID = 1.4 / math.sqrt(62.0)
EPSILON = 1e-05
NEGATIVE = -1e30
SCORE = 1.0 / math.sqrt(NOPE + ROPE)

F32 = jnp.float32
BF16 = jnp.bfloat16

LATENT = QRANK + KVRANK
LAT_COLS = LATENT + LANES
LOW_ROWS = LAT_COLS - QRANK


def round_up(size, unit):
    return -(-size // unit) * unit


def product(left, right):
    return jnp.dot(left, right, preferred_element_type=F32)


def times_transposed(left, right):
    return lax.dot_general(left, right, (((1,), (1,)), ((), ())), preferred_element_type=F32)


def transposed_times(left, right):
    return lax.dot_general(left, right, (((0,), (0,)), ((), ())), preferred_element_type=F32)


def rotary_tables(positions):
    exponent = jnp.arange(0, ROPE, 2, dtype=F32) / ROPE
    inverse = 1.0 / 10000.0**exponent
    angles = positions[:, None] * inverse[None, :]
    angles = jnp.concatenate([angles, angles], axis=1)
    return (jnp.cos(angles), jnp.sin(angles))


def lane_tables(cos_table, sin_table):
    rows = cos_table.shape[0]
    half = ROPE // 2
    ones = jnp.ones((rows, NOPE), F32)
    before = jnp.zeros((rows, NOPE), F32)
    after = jnp.zeros((rows, LANES - NOPE - ROPE), F32)
    gap = jnp.zeros((rows, half), F32)
    return (
        jnp.concatenate([ones, cos_table, after], axis=1),
        jnp.concatenate([before, -sin_table[:, :half], gap, after], axis=1),
        jnp.concatenate([before, gap, sin_table[:, half:], after], axis=1),
    )


def turn_lanes(values, cos_table, lower_table, upper_table, sign):
    return (
        values * cos_table
        + sign * (pltpu.roll(values, LANES - ROPE // 2, 1) * lower_table)
        + sign * (pltpu.roll(values, ROPE // 2, 1) * upper_table)
    )


def swap(value, axis, distance):
    size = lax.axis_size(axis)
    return lax.ppermute(value, axis, [(i, i ^ distance) for i in range(size)])


def together(*arrays):
    count = len(arrays)
    return pl.pallas_call(
        lambda *refs: None,
        in_specs=[pl.BlockSpec(memory_space=pl.ANY)] * count,
        out_specs=[pl.BlockSpec(memory_space=pl.ANY)] * count,
        out_shape=[jax.ShapeDtypeStruct(a.shape, a.dtype) for a in arrays],
        input_output_aliases={i: i for i in range(count)},
        name="together",
    )(*arrays)


def in_turn(operands, order, move):
    operands = dict(operands)
    arrived = {}
    before = []
    for group in order:
        if before:
            both = together(*[operands[name] for name in group], *[arrived[name] for name in before])
            for name, array in zip(group, both[: len(group)]):
                operands[name] = array
            for name, array in zip(before, both[len(group) :]):
                arrived[name] = array
        for name in group:
            arrived[name] = move(name, operands[name])
        before = group
    return operands, arrived


def spread_ctx(own):
    first = swap(own, "ctx", 1)
    second = swap(own, "ctx", 2)
    return [own, first, second, swap(second, "ctx", 1)]


def exchange_ctx(chunks):
    return [chunks[0]] + [swap(chunks[k], "ctx", k) for k in range(1, len(chunks))]


def sum_ctx(parts):
    third = swap(parts[3].astype(BF16), "ctx", 1)
    far = (parts[2].astype(F32) + third.astype(F32)).astype(BF16)
    near = swap(parts[1].astype(BF16), "ctx", 1)
    return parts[0].astype(F32) + near.astype(F32) + swap(far, "ctx", 2).astype(F32)


def spread_tp(own):
    far = swap(own, "tp", 2)
    return [own, swap(own, "tp", 1), far, swap(far, "tp", 1)]


def total_tp(value):
    value = value + swap(value, "tp", 1)
    return value + swap(value, "tp", 2)


def fold_halves(keep, send):
    pair = (keep + swap(send, "tp", 1)).astype(BF16)
    mine = pair.astype(F32) + swap(pair, "tp", 2).astype(F32)
    return mine, swap(mine, "tp", 1)


def at_once(copies):
    for copy in copies:
        copy.start()
    for copy in copies:
        copy.wait()


def shard_place(where, index, n_ctx):
    return (where[0] ^ (index // n_ctx)) * n_ctx + (where[1] ^ (index % n_ctx))


def row_copies(where, pieces, first_row, rows, target, sems, first_sem, n_ctx):
    if len(pieces) == 1:
        return [pltpu.make_async_copy(pieces[0], target, sems.at[first_sem])]
    out = []
    for index, piece in enumerate(pieces):
        start = pl.multiple_of(shard_place(where, index, n_ctx) * rows, SUBLANES)
        out.append(
            pltpu.make_async_copy(
                piece.at[pl.ds(first_row, rows), :],
                target.at[pl.ds(start, rows), :],
                sems.at[first_sem + index],
            )
        )
    return out


def feature_start(where, place, width):
    return pl.multiple_of((where[2] ^ place) * width, LANES)


def feature_copies(where, pieces, target, row, rows, width, sems, first_sem):
    return [
        pltpu.make_async_copy(
            piece,
            target.at[pl.ds(row, rows), pl.ds(feature_start(where, place, width), width)],
            sems.at[first_sem + place],
        )
        for place, piece in enumerate(pieces)
    ]


def run_kernel(body, inputs, outputs, scratch, flops, moved, name, grid=None, exps=0, waits=()):
    count = len(inputs)
    inputs = list(inputs) + [(array, ANY) for array in waits]

    def used(*refs):
        body(*refs[:count], *refs[len(inputs) :])

    return pl.pallas_call(
        used,
        grid=grid if grid is not None else (),
        in_specs=[spec for _, spec in inputs],
        out_specs=[spec for _, spec in outputs],
        out_shape=[shape for shape, _ in outputs],
        scratch_shapes=scratch,
        compiler_params=pltpu.CompilerParams(vmem_limit_bytes=56 << 20),
        cost_estimate=pl.CostEstimate(flops=flops, bytes_accessed=moved, transcendentals=exps),
        name=name,
    )(*[array for array, _ in inputs])


VMEM = pl.BlockSpec(memory_space=pltpu.VMEM)
SMEM = pl.BlockSpec(memory_space=pltpu.SMEM)
ANY = pl.BlockSpec(memory_space=pl.ANY)


def shape(dims, dtype=BF16):
    return jax.ShapeDtypeStruct(dims, dtype)


def cut_hidden(where, gate, up, down, parts=1, waits=()):
    rows, total = gate.shape
    hidden = total // 4
    columns = round_up(3 * hidden, LANES)

    def body(where_ref, gate_ref, up_ref, down_ref, *rest):
        outs, stage = rest[:-1], rest[-1]
        blank = jnp.zeros((rows, columns - 3 * hidden), BF16)
        for place in range(4):
            units = slice(place * hidden, (place + 1) * hidden)
            stage[place] = jnp.concatenate(
                [gate_ref[:, units], up_ref[:, units], down_ref[:, units], blank], axis=1
            )
        for number, out in enumerate(outs):
            first = number // 4 * (rows // parts)
            out[...] = stage[where_ref[1] ^ (number % 4), first : first + rows // parts]

    return run_kernel(
        body,
        [(where, SMEM), (gate, VMEM), (up, VMEM), (down.T, VMEM)],
        [(shape((rows // parts, columns)), VMEM)] * (4 * parts),
        [pltpu.VMEM((4, rows, columns), BF16)],
        0,
        12 * rows * total,
        "cut_hidden",
        waits=waits,
    )


def join_hidden(where, pieces, hidden, waits=()):
    rows = pieces[0].shape[0]

    def body(where_ref, p0, p1, p2, p3, gate_ref, up_ref, down_ref, stage):
        for step, piece in enumerate((p0, p1, p2, p3)):
            stage[where_ref[1] ^ step] = piece[...]
        for first, out in ((0, gate_ref), (hidden, up_ref), (2 * hidden, down_ref)):
            out[...] = jnp.concatenate(
                [stage[place][:, first : first + hidden].astype(F32) for place in range(4)], axis=1
            )

    return run_kernel(
        body,
        [(where, SMEM)] + [(piece, VMEM) for piece in pieces],
        [
            (shape((rows, 4 * hidden), F32), VMEM),
            (shape((rows, 4 * hidden), F32), VMEM),
            (shape((rows, 4 * hidden), F32), VMEM),
        ],
        [pltpu.VMEM((4,) + pieces[0].shape, BF16)],
        0,
        80 * rows * hidden,
        "join_hidden",
        waits=waits,
    )


def latent_products(
    where, normed, pick, query_pieces, low_pieces, query_rows, low_rows, first_low, n_ctx, paired, waits=()
):
    rows, width = normed.shape
    half = rows // 2
    shared = query_pieces is low_pieces
    shards = len(query_pieces)
    arrays = list(query_pieces) if shared else list(query_pieces) + list(low_pieces)

    def body(where_ref, normed_ref, pick_ref, *rest):
        refs = rest[: len(arrays)]
        keep, send, joined, query_gain, latent_gain, low_in, total, sems = rest[len(arrays) :]
        query_refs = refs[: len(query_pieces)]
        low_refs = query_refs if shared else refs[len(query_pieces) :]
        copies = row_copies(
            where_ref, query_refs, 0, query_rows, joined.at[pl.ds(0, QRANK), :], sems, 0, n_ctx
        )
        copies += row_copies(
            where_ref, low_refs, first_low, low_rows, low_in, sems, len(query_refs), n_ctx
        )
        at_once(copies)
        joined[QRANK:, :] = product(pick_ref[...], low_in[...]).astype(BF16)
        if paired:
            first = LATENT + ROPE
            pieces = joined[first : first + SUBLANES, :LANES].astype(F32)
            query_gain[...] = jnp.concatenate(
                [pieces[i : i + 1, :query_rows] for i in range(shards)], axis=1
            )
            latent_gain[...] = jnp.concatenate(
                [pieces[i : i + 1, query_rows:] for i in range(shards)], axis=1
            )
            joined[first : first + SUBLANES, :] = jnp.zeros((SUBLANES, width), BF16)
        total[...] = times_transposed(normed_ref[...], joined[...])
        core = where_ref[3]
        keep[...] = total[pl.ds(pl.multiple_of(core * half, 8), half), :]
        send[...] = total[pl.ds(pl.multiple_of((1 - core) * half, 8), half), :]

    return run_kernel(
        body,
        [(where, SMEM), (normed, VMEM), (pick, VMEM)] + [(a, ANY) for a in arrays],
        [
            (shape((half, LAT_COLS), F32), VMEM),
            (shape((half, LAT_COLS), F32), VMEM),
            (shape((LAT_COLS, width)), VMEM),
            (shape((1, QRANK), F32), VMEM),
            (shape((1, KVRANK), F32), VMEM),
        ],
        [
            pltpu.VMEM((pick.shape[1], width), BF16),
            pltpu.VMEM((rows, LAT_COLS), F32),
            pltpu.SemaphoreType.DMA((len(query_pieces) + len(low_pieces),)),
        ],
        2 * rows * width * LAT_COLS,
        8 << 20,
        "latent_products",
        waits=waits,
    )


def latent_norms(where, mine, other, gain_query, gain_latent, tables, waits=()):
    half = mine.shape[0]
    rows = 2 * half

    def body(where_ref, mine_ref, other_ref, gq, gl, cos_t, lower_t, upper_t, latent, query_low, payload):
        core = where_ref[3]
        latent[pl.ds(pl.multiple_of(core * half, 8), half), :] = mine_ref[...]
        latent[pl.ds(pl.multiple_of((1 - core) * half, 8), half), :] = other_ref[...]
        query = latent[:, :QRANK]
        inverse = lax.rsqrt(jnp.mean(query * query, axis=1, keepdims=True) + EPSILON)
        query_low[...] = (query * inverse * gq[...]).astype(BF16)
        low = latent[:, QRANK:LATENT]
        inverse = lax.rsqrt(jnp.mean(low * low, axis=1, keepdims=True) + EPSILON)
        payload[:, :KVRANK] = (low * inverse * gl[...]).astype(BF16)
        rope = pltpu.roll(latent[:, LATENT:], NOPE, 1)
        payload[:, KVRANK:] = turn_lanes(rope, cos_t[...], lower_t[...], upper_t[...], 1.0).astype(BF16)

    return run_kernel(
        body,
        [(where, SMEM)]
        + [(a, VMEM) for a in (mine, other, gain_query, gain_latent) + tables],
        [
            (shape((rows, LAT_COLS), F32), VMEM),
            (shape((rows, QRANK)), VMEM),
            (shape((rows, KVRANK + LANES)), VMEM),
        ],
        [],
        20 * rows * LAT_COLS,
        4 << 20,
        "latent_norms",
        waits=waits,
    )


def masked_blocks(scores, place, rows, blocks):
    key_row = lax.broadcasted_iota(jnp.int32, (rows, rows), 0)
    query_column = lax.broadcasted_iota(jnp.int32, (rows, rows), 1)
    out = [jnp.where(key_row <= query_column, scores[:rows], NEGATIVE)]
    for block in range(1, blocks):
        seen = (place ^ block) < place
        out.append(jnp.where(seen, scores[block * rows : (block + 1) * rows], NEGATIVE))
    return out


def head_lanes(index):
    return pl.ds(pl.multiple_of(index * 2 * LANES, 2 * LANES), 2 * LANES)


def up_copies(where_ref, refs, wq, wkv, sems, n_ctx):
    if len(refs) == 3:
        return [
            pltpu.make_async_copy(refs[0], wq, sems.at[0]),
            pltpu.make_async_copy(refs[1], wkv, sems.at[1]),
        ]
    shards = len(refs) // 2
    query_rows = QRANK // shards
    low_rows = KVRANK // shards
    refs = refs[:shards]
    return row_copies(where_ref, refs, 0, query_rows, wq, sems, 0, n_ctx) + row_copies(
        where_ref, refs, query_rows, low_rows, wkv, sems, shards, n_ctx
    )


def out_copies(where_ref, refs, target, sems, first_sem, n_ctx):
    if len(refs) == 3:
        return [pltpu.make_async_copy(refs[2], target, sems.at[first_sem])]
    refs = refs[len(refs) // 2 :]
    return row_copies(where_ref, refs, 0, refs[0].shape[0], target, sems, first_sem, n_ctx)


def sequence_refs(source):
    return [piece for group in source for piece in group]


def sequence_shape(source):
    return (4 * len(source),) + source[0][0].shape


def sequence_copies(where, refs, target, rows, width, sems, first_sem):
    return [
        feature_copies(
            where, refs[at : at + 4], target, at // 4 * rows, rows, width, sems, first_sem + at
        )
        for at in range(0, len(refs), 4)
    ]


def hidden_copies(where, arrays, target, sems, first_sem, n_ctx, columns=None):
    cut = (lambda ref: ref) if columns is None else (lambda ref: ref.at[:, columns])
    if len(arrays) == 1:
        return [pltpu.make_async_copy(cut(arrays[0]), target, sems.at[first_sem])]
    rows = arrays[0].shape[0]
    parts = target.shape[0] // (rows * 2 * n_ctx)
    out = []
    for number, ref in enumerate(arrays):
        part, index = number // (2 * n_ctx), number % (2 * n_ctx)
        start = shard_place(where, index, n_ctx) * parts + part
        start = pl.multiple_of(start * rows, SUBLANES)
        out.append(
            pltpu.make_async_copy(
                cut(ref), target.at[pl.ds(start, rows), :], sems.at[first_sem + number]
            )
        )
    return out


def attention_forward(where, query_low, payloads, ups, tables, heads, n_ctx, waits=()):
    rows = query_low.shape[0]
    blocks = len(payloads)
    keys = blocks * rows
    pairs = heads // 2
    whole = lambda dims: pl.BlockSpec(dims, lambda i: (0, 0))
    column = lambda dims: pl.BlockSpec(dims, lambda i: (0, i))

    def body(where_ref, low_q, cos_t, lower_t, upper_t, *rest):
        sources = rest[:blocks]
        up_refs = rest[blocks : blocks + len(ups)]
        out, q_out, kv_out, lse_out, wq, wkv, tokens, sems = rest[blocks + len(ups) :]
        step = pl.program_id(0)

        @pl.when(step == 0)
        def _():
            copies = up_copies(where_ref, up_refs, wq, wkv, sems, n_ctx)
            first = len(copies)
            for block, source in enumerate(sources):
                copies.append(
                    pltpu.make_async_copy(
                        source, tokens.at[pl.ds(block * rows, rows), :], sems.at[first + block]
                    )
                )
            at_once(copies)

        key_lane = lax.broadcasted_iota(jnp.int32, (keys, LANES), 1)
        raw_pair = product(low_q[...], wq[:, head_lanes(step)])
        kv_pair = product(tokens[:, :KVRANK], wkv[:, head_lanes(step)]).astype(BF16)
        rope_key = tokens[:, KVRANK:]
        kv_out[...] = kv_pair
        outs = []
        for head in range(2):
            lanes = slice(head * LANES, (head + 1) * LANES)
            query = turn_lanes(
                raw_pair[:, lanes], cos_t[...], lower_t[...], upper_t[...], 1.0
            ).astype(BF16)
            pair = kv_pair[:, lanes]
            key = jnp.where(key_lane < NOPE, pair, rope_key)
            q_out[:, lanes] = query
            scores = times_transposed(key, query) * SCORE
            masked = masked_blocks(scores, where_ref[1], rows, blocks)
            top = functools.reduce(
                jnp.maximum, [jnp.max(part, axis=0, keepdims=True) for part in masked]
            )
            powers = [jnp.exp(part - top) for part in masked]
            total = sum(jnp.sum(part, axis=0, keepdims=True) for part in powers)
            prob = jnp.concatenate([part.astype(BF16) for part in powers], axis=0)
            mixed = transposed_times(pair, prob) / total
            outs.append(jnp.transpose(mixed))
            lse_out[0, head : head + 1, :] = top + jnp.log(total)
        lane = lax.broadcasted_iota(jnp.int32, (rows, LANES), 1)
        out[...] = jnp.where(lane < VDIM, pltpu.roll(outs[0], VDIM, 1), outs[1]).astype(BF16)

    return run_kernel(
        body,
        [(where, SMEM), (query_low, whole(query_low.shape))]
        + [(table, whole(table.shape)) for table in tables]
        + [(a, ANY) for a in list(payloads) + list(ups)],
        [
            (shape((rows, pairs * LANES)), column((rows, LANES))),
            (shape((rows, heads * LANES)), column((rows, 2 * LANES))),
            (shape((keys, heads * LANES)), column((keys, 2 * LANES))),
            (shape((pairs, 8, rows), F32), pl.BlockSpec((1, 8, rows), lambda i: (i, 0, 0))),
        ],
        [
            pltpu.VMEM((QRANK, heads * LANES), BF16),
            pltpu.VMEM((KVRANK, heads * LANES), BF16),
            pltpu.VMEM((keys, KVRANK + LANES), BF16),
            pltpu.SemaphoreType.DMA((64 + blocks,)),
        ],
        2 * heads * rows * (QRANK + 2 * keys) * LANES + 2 * heads * keys * KVRANK * LANES,
        12 << 20,
        "attention_forward",
        grid=(pairs,),
        exps=heads * rows * keys,
        waits=waits,
    )


def attention_backward(where, queries, pairs_low, lse, payloads, ups, branch, tables, n_ctx, waits=()):
    rows, q_lanes = queries.shape
    heads = q_lanes // LANES
    pairs = heads // 2
    blocks = len(payloads)
    keys = blocks * rows
    width = branch[0].shape[1]
    full_width = 4 * width
    inner = heads * VDIM
    whole = lambda dims: pl.BlockSpec(dims, lambda i: (0, 0))
    column = lambda dims: pl.BlockSpec(dims, lambda i: (0, i))
    moved = list(payloads) + list(ups) + list(branch)

    def body(where_ref, q_in, kv_in, lse_in, cos_t, lower_t, upper_t, *rest):
        refs = rest[: len(moved)]
        (dq_out, dkv_out, query_sum, kv_keep, kv_1, kv_2, kv_3) = rest[len(moved) : len(moved) + 7]
        wq, wkv, rope_key, wo, grad_in, dout, kv_sum, sems = rest[len(moved) + 7 :]
        step = pl.program_id(0)
        place = where_ref[1]

        @pl.when(step == 0)
        def _():
            at = 0
            sources, at = refs[at : at + blocks], at + blocks
            up_refs, at = refs[at : at + len(ups)], at + len(ups)
            branch_refs = refs[at : at + 4]
            copies = up_copies(where_ref, up_refs, wq, wkv, sems, n_ctx)
            for block, source in enumerate(sources):
                copies.append(
                    pltpu.make_async_copy(
                        source.at[:, pl.ds(KVRANK, LANES)],
                        rope_key.at[pl.ds(block * rows, rows), :],
                        sems.at[len(copies)],
                    )
                )
            copies += feature_copies(
                where_ref, branch_refs, grad_in, 0, rows, width, sems, len(copies)
            )
            copies += out_copies(where_ref, up_refs, wo, sems, len(copies), n_ctx)
            at_once(copies)
            dout[...] = product(grad_in[...], wo[...]).astype(BF16).astype(F32)
            query_sum[...] = jnp.zeros_like(query_sum)
            kv_sum[...] = jnp.zeros_like(kv_sum)

        key_lane = lax.broadcasted_iota(jnp.int32, (keys, LANES), 1)
        lane = lax.broadcasted_iota(jnp.int32, (rows, LANES), 1)
        both = dout[:, pl.ds(pl.multiple_of(step * LANES, LANES), LANES)]
        dkr = jnp.zeros((keys, LANES), F32)
        dq_parts = []
        dkv_parts = []
        for head in range(2):
            lanes = slice(head * LANES, (head + 1) * LANES)
            query = q_in[:, lanes]
            pair = kv_in[:, lanes]
            key = jnp.where(key_lane < NOPE, pair, rope_key[...])
            upper = pltpu.roll(both, VDIM, 1) if head == 0 else both
            out_grad = jnp.where(lane >= NOPE, upper, 0.0).astype(BF16)
            scores = times_transposed(key, query) * SCORE
            top = lse_in[0, head : head + 1, :]
            masked = masked_blocks(scores, place, rows, blocks)
            prob = jnp.concatenate([jnp.exp(part - top) for part in masked], axis=0)
            prob_grad = times_transposed(pair, out_grad)
            weighted = prob * prob_grad
            delta = jnp.sum(weighted, axis=0, keepdims=True)
            score_grad = (weighted - prob * delta).astype(BF16)
            key_grad = product(score_grad, query) * SCORE
            value_grad = product(prob.astype(BF16), out_grad)
            dkv_parts.append(jnp.where(key_lane < NOPE, key_grad, value_grad).astype(BF16))
            dkr = dkr + key_grad
            query_grad = jnp.transpose(transposed_times(key, score_grad)) * SCORE
            dq_parts.append(
                turn_lanes(query_grad, cos_t[...], lower_t[...], upper_t[...], -1.0).astype(BF16)
            )
        dq_pair = jnp.concatenate(dq_parts, axis=1)
        dkv_pair = jnp.concatenate(dkv_parts, axis=1)
        dq_out[...] = dq_pair
        dkv_out[...] = dkv_pair
        query_sum[...] += times_transposed(dq_pair, wq[:, head_lanes(step)])
        kv_sum[:, :KVRANK] += times_transposed(dkv_pair, wkv[:, head_lanes(step)])
        kv_sum[:, KVRANK:] += jnp.where(key_lane >= NOPE, dkr, 0.0)

        @pl.when(step == pairs - 1)
        def _():
            kv_keep[...] = kv_sum[:rows]
            for block, out in ((1, kv_1), (2, kv_2), (3, kv_3)):
                out[...] = kv_sum[block * rows : (block + 1) * rows].astype(BF16)

    return run_kernel(
        body,
        [
            (where, SMEM),
            (queries, column((rows, 2 * LANES))),
            (pairs_low, column((keys, 2 * LANES))),
            (lse, pl.BlockSpec((1, 8, rows), lambda i: (i, 0, 0))),
        ]
        + [(table, whole(table.shape)) for table in tables]
        + [(a, ANY) for a in moved],
        [
            (shape((rows, heads * LANES)), column((rows, 2 * LANES))),
            (shape((keys, heads * LANES)), column((keys, 2 * LANES))),
            (shape((rows, QRANK), F32), whole((rows, QRANK))),
            (shape((rows, KVRANK + LANES), F32), whole((rows, KVRANK + LANES))),
        ]
        + [(shape((rows, KVRANK + LANES)), whole((rows, KVRANK + LANES)))] * 3,
        [
            pltpu.VMEM((QRANK, heads * LANES), BF16),
            pltpu.VMEM((KVRANK, heads * LANES), BF16),
            pltpu.VMEM((keys, LANES), BF16),
            pltpu.VMEM((full_width, inner), BF16),
            pltpu.VMEM((rows, full_width), BF16),
            pltpu.VMEM((rows, inner), F32),
            pltpu.VMEM((keys, KVRANK + LANES), F32),
            pltpu.SemaphoreType.DMA((128 + blocks,)),
        ],
        10 * heads * rows * keys * LANES,
        24 << 20,
        "attention_backward",
        grid=(pairs,),
        exps=heads * rows * keys,
        waits=waits,
    )


def output_products(where, attended, ups, full_width, n_ctx, waits=()):
    rows, inner = attended.shape
    count = len(ups)
    width = full_width // 4

    def body(where_ref, attended_ref, *rest):
        refs = rest[:count]
        keep, send, weight, sems = rest[count:]
        at_once(out_copies(where_ref, refs, weight, sems, 0, n_ctx))
        for place in range(4):
            block = weight[pl.ds(feature_start(where_ref, place, width), width), :]
            part = times_transposed(attended_ref[...], block)
            if place % 2 == 0:
                keep[place // 2] = part
            else:
                send[place // 2] = part.astype(BF16)

    return run_kernel(
        body,
        [(where, SMEM), (attended, VMEM)] + [(a, ANY) for a in ups],
        [(shape((2, rows, width), F32), VMEM), (shape((2, rows, width)), VMEM)],
        [pltpu.VMEM((full_width, inner), BF16), pltpu.SemaphoreType.DMA((64,))],
        2 * rows * inner * full_width,
        6 << 20,
        "output_products",
        waits=waits,
    )


def feed_forward(where, tokens, branches, weights, gains, hidden, n_ctx):
    count, rows, width = sequence_shape(tokens)
    blocks = count // 4
    full_width = 4 * width
    columns = weights[0].shape[-1]
    upper_end = round_up(2 * hidden, LANES)
    lower_start = 2 * hidden // LANES * LANES
    shift = 2 * hidden - lower_start
    lower_cols = columns - lower_start
    total = blocks * rows
    token_list, branch_list = sequence_refs(tokens), sequence_refs(branches)
    flat = len(token_list) + len(branch_list)
    moved = token_list + branch_list + list(gains) + list(weights)

    def body(where_ref, *rest):
        refs = rest[: len(moved)]
        pairs_out, active_out, keep, send, inverse_out = rest[len(moved) : len(moved) + 5]
        normed, branch, weight, gain, sems = rest[len(moved) + 5 :]
        first = 2 * count
        weight_copies = feature_copies(
            where_ref, refs[flat : flat + 4], gain, 0, gain.shape[0], width, sems, first
        ) + hidden_copies(where_ref, refs[flat + 4 :], weight, sems, first + 4, n_ctx)
        token_copies = [
            first_list + second_list
            for first_list, second_list in zip(
                sequence_copies(
                    where_ref, refs[: len(token_list)], normed, rows, width, sems, 0
                ),
                sequence_copies(
                    where_ref, refs[len(token_list) : flat], branch, rows, width, sems, count
                ),
            )
        ]
        for copy in weight_copies + sum(token_copies, []):
            copy.start()
        for copy in weight_copies:
            copy.wait()

        def hidden_block(block, carry):
            for number, copies in enumerate(token_copies):

                @pl.when(block == number)
                def _():
                    for copy in copies:
                        copy.wait()

            here = pl.ds(pl.multiple_of(block * rows, rows), rows)
            source = normed[here, :].astype(F32) / gain[:1, :]
            inverse = lax.rsqrt(jnp.mean(source * source, axis=1, keepdims=True) + EPSILON)

            @pl.when(block == 0)
            def _():
                inverse_out[...] = jnp.broadcast_to(inverse, inverse_out.shape)

            both = product(normed[here, :], weight[:, :upper_end]) * inverse
            lower = product(branch[here, :], weight[:, lower_start:])
            gate = both[:, :hidden]
            upper = both[:, hidden : 2 * hidden]
            grad = lower[:, shift : shift + hidden]
            scaled = grad * inverse
            sigmoid = 1.0 / (1.0 + jnp.exp(-gate))
            active = gate * sigmoid
            pairs_out[here, :] = jnp.concatenate(
                [
                    scaled * upper * sigmoid * (1.0 + gate * (1.0 - sigmoid)),
                    scaled * active,
                    jnp.zeros((rows, upper_end - 2 * hidden), F32),
                ],
                axis=1,
            ).astype(BF16)
            active_out[here, :] = jnp.concatenate(
                [
                    jnp.zeros((rows, shift), F32),
                    active * upper,
                    jnp.zeros((rows, lower_cols - shift - hidden), F32),
                ],
                axis=1,
            ).astype(BF16)
            return carry

        lax.fori_loop(0, blocks, hidden_block, 0)
        for place in range(4):
            block = weight[pl.ds(feature_start(where_ref, place, width), width), :upper_end]
            part = times_transposed(pairs_out[...], block).astype(BF16)
            (send if place % 2 else keep)[place // 2] = part

    return run_kernel(
        body,
        [(where, SMEM)] + [(a, ANY) for a in moved],
        [
            (shape((total, upper_end)), VMEM),
            (shape((total, lower_cols)), VMEM),
            (shape((2, total, width)), VMEM),
            (shape((2, total, width)), VMEM),
            (shape((rows, LANES), F32), VMEM),
        ],
        [
            pltpu.VMEM((total, full_width), BF16),
            pltpu.VMEM((total, full_width), BF16),
            pltpu.VMEM((full_width, columns), BF16),
            pltpu.VMEM(gains[0].shape[:1] + (full_width,), F32),
            pltpu.SemaphoreType.DMA((2 * count + 4 + full_width // SUBLANES,)),
        ],
        10 * total * full_width * hidden,
        28 << 20,
        "feed_forward",
        exps=total * hidden,
    )


def feed_forward_result(where, active, weights, hidden, n_ctx, waits=()):
    total, lower_cols = active.shape
    columns = weights[0].shape[1]
    full_width = sum(a.shape[0] for a in weights)
    width = full_width // 4
    count = len(weights)

    def body(where_ref, active_ref, *rest):
        refs = rest[:count]
        outs = rest[count:-2]
        weight, sems = rest[-2:]
        lower = pl.ds(columns - lower_cols, lower_cols)
        at_once(hidden_copies(where_ref, refs, weight, sems, 0, n_ctx, columns=lower))
        for place in range(4):
            block = weight[pl.ds(feature_start(where_ref, place, width), width), :]
            part = times_transposed(active_ref[...], block).astype(BF16)
            outs[place % 2][place // 2] = part

    return run_kernel(
        body,
        [(where, SMEM), (active, VMEM)] + [(a, ANY) for a in weights],
        [(shape((2, total, width)), VMEM)] * 2,
        [
            pltpu.VMEM((full_width, lower_cols), BF16),
            pltpu.SemaphoreType.DMA((full_width // SUBLANES,)),
        ],
        2 * total * full_width * hidden,
        10 << 20,
        "feed_forward_result",
        waits=waits,
    )


def feed_forward_grads(
    where, tokens, branches, pairs_grad, active, hidden, columns, shards, n_ctx, distance, waits=()
):
    count, rows, width = sequence_shape(tokens)
    token_list, branch_list = sequence_refs(tokens), sequence_refs(branches)
    total = count // 4 * rows
    upper_end = pairs_grad.shape[1]
    lower_cols = active.shape[1]
    lower_start = columns - lower_cols
    shard_rows = 4 * width // shards

    def gradient(normed, branch, pairs_ref, active_ref):
        first = transposed_times(normed, pairs_ref[...])
        second = transposed_times(branch, active_ref[...])
        middle = first[:, lower_start:] + second[:, : upper_end - lower_start]
        return jnp.concatenate(
            [first[:, :lower_start], middle, second[:, upper_end - lower_start :]], axis=1
        ).astype(BF16)

    def body(where_ref, pairs_ref, active_ref, *rest):
        token_refs, rest = rest[: len(token_list)], rest[len(token_list) :]
        branch_refs, rest = rest[: len(branch_list)], rest[len(branch_list) :]
        outs = rest[:-4]
        normed, branch, stage, sems = rest[-4:]
        copies = sequence_copies(where_ref, token_refs, normed, rows, width, sems, 0)
        copies += sequence_copies(where_ref, branch_refs, branch, rows, width, sems, count)
        at_once(sum(copies, []))
        if distance is None:
            for place in range(4):
                here = slice(place * width, (place + 1) * width)
                outs[0][here, :] = gradient(normed[:, here], branch[:, here], pairs_ref, active_ref)
            return
        for number in range(n_ctx // 2):
            place = owner_blocks(where_ref, distance * (n_ctx // 2) + number, n_ctx)
            here = pl.ds(pl.multiple_of(place * width, LANES), width)
            stage[...] = gradient(normed[:, here], branch[:, here], pairs_ref, active_ref)
            for low in range(2):
                start = pl.multiple_of((low ^ (where_ref[1] % 2)) * shard_rows, SUBLANES)
                outs[2 * number + low][...] = stage[pl.ds(start, shard_rows), :]

    if distance is None:
        outputs = [(shape((4 * width, columns)), VMEM)]
    else:
        outputs = [(shape((shard_rows, columns)), VMEM)] * n_ctx
    return run_kernel(
        body,
        [(where, SMEM), (pairs_grad, VMEM), (active, VMEM)]
        + [(a, ANY) for a in token_list + branch_list],
        outputs,
        [
            pltpu.VMEM((total, 4 * width), BF16),
            pltpu.VMEM((total, 4 * width), BF16),
            pltpu.VMEM((width, columns), BF16),
            pltpu.SemaphoreType.DMA((2 * count,)),
        ],
        6 * total * 4 * width * hidden // 2,
        18 << 20,
        "feed_forward_grads",
        waits=waits,
    )


def owner_blocks(where_ref, part, n_ctx):
    per_row = n_ctx // 2
    return (where_ref[0] ^ (part // per_row)) * per_row + ((where_ref[1] // 2) ^ (part % per_row))


def output_grads(where, attended, branch, shards, n_ctx, paired, waits=()):
    rows, inner = attended.shape
    width = branch[0].shape[1]
    shard_rows = 4 * width // shards

    def body(where_ref, attended_ref, b0, b1, b2, b3, *rest):
        outs = rest[:-3]
        grad_in, stage, sems = rest[-3:]
        at_once(feature_copies(where_ref, (b0, b1, b2, b3), grad_in, 0, rows, width, sems, 0))
        for part in range(4):
            place = owner_blocks(where_ref, part, n_ctx) if paired else part
            here = pl.ds(pl.multiple_of(place * width, LANES), width)
            stage[...] = transposed_times(grad_in[:, here], attended_ref[...]).astype(BF16)
            if not paired:
                outs[0][part * width : (part + 1) * width, :] = stage[...]
                continue
            for low in range(2):
                start = pl.multiple_of((low ^ (where_ref[1] % 2)) * shard_rows, SUBLANES)
                outs[2 * part + low][...] = stage[pl.ds(start, shard_rows), :]

    if paired:
        outputs = [(shape((shard_rows, inner)), VMEM)] * shards
    else:
        outputs = [(shape((4 * width, inner)), VMEM)]
    return run_kernel(
        body,
        [(where, SMEM), (attended, VMEM)] + [(a, ANY) for a in branch],
        outputs,
        [
            pltpu.VMEM((rows, 4 * width), BF16),
            pltpu.VMEM((width, inner), BF16),
            pltpu.SemaphoreType.DMA((4,)),
        ],
        2 * rows * inner * 4 * width,
        6 << 20,
        "output_grads",
        waits=waits,
    )


def up_grads(where, query_low, query_grad, payloads, pair_grad, shards, n_ctx, paired, waits=()):
    rows = query_low.shape[0]
    blocks = len(payloads)
    lanes = query_grad.shape[1]
    query_rows = QRANK // shards
    low_rows = KVRANK // shards

    def body(where_ref, low_q, dq, dkv, *rest):
        sources = rest[:blocks]
        rest = rest[blocks:]
        outs = rest[:-4]
        tokens, stage_q, stage_kv, sems = rest[-4:]
        at_once(
            [
                pltpu.make_async_copy(
                    source.at[:, pl.ds(0, KVRANK)],
                    tokens.at[pl.ds(block * rows, rows), :],
                    sems.at[block],
                )
                for block, source in enumerate(sources)
            ]
        )
        grad_q = transposed_times(low_q[...], dq[...]).astype(BF16)
        grad_kv = transposed_times(tokens[...], dkv[...]).astype(BF16)
        if not paired:
            outs[0][...] = grad_q
            outs[1][...] = grad_kv
            return
        stage_q[...] = grad_q
        stage_kv[...] = grad_kv
        for index, out in enumerate(outs):
            place = shard_place(where_ref, index, n_ctx)
            out[:query_rows, :] = stage_q[
                pl.ds(pl.multiple_of(place * query_rows, SUBLANES), query_rows), :
            ]
            out[query_rows:, :] = stage_kv[
                pl.ds(pl.multiple_of(place * low_rows, SUBLANES), low_rows), :
            ]

    if paired:
        outputs = [(shape((query_rows + low_rows, lanes)), VMEM)] * shards
    else:
        outputs = [(shape((QRANK, lanes)), VMEM), (shape((KVRANK, lanes)), VMEM)]
    return run_kernel(
        body,
        [(where, SMEM), (query_low, VMEM), (query_grad, VMEM), (pair_grad, VMEM)]
        + [(a, ANY) for a in payloads],
        outputs,
        [
            pltpu.VMEM((blocks * rows, KVRANK), BF16),
            pltpu.VMEM((QRANK, lanes), BF16),
            pltpu.VMEM((KVRANK, lanes), BF16),
            pltpu.SemaphoreType.DMA((blocks,)),
        ],
        2 * lanes * (rows * QRANK + blocks * rows * KVRANK),
        10 << 20,
        "up_grads",
        waits=waits,
    )


def input_backward(
    where,
    mine,
    other,
    latent,
    gain_query,
    gain_latent,
    tables,
    normed,
    joined,
    activations,
    inverse_one,
    gain_one,
    middle_grad,
    pick,
    query_rows,
    low_rows,
    shards,
    n_ctx,
    paired,
    waits=(),
):
    half = mine.shape[0]
    rows, width = normed.shape
    full_width = 4 * width
    low_in = pick.shape[1]

    def body(
        where_ref, mine_ref, other_ref, latent_ref, gq, gl, cos_t, lower_t, upper_t, normed_ref,
        joined_ref, act_ref, inverse_ref, gain_ref, middle_ref, pick_ref, input_out, query_gain_out,
        latent_gain_out, gain_out, *rest
    ):
        outs = rest[:-3]
        sums, stage_q, stage_low = rest[-3:]
        core = where_ref[3]
        sums[pl.ds(pl.multiple_of(core * half, 8), half), :] = mine_ref[...]
        sums[pl.ds(pl.multiple_of((1 - core) * half, 8), half), :] = other_ref[...]
        parts = []
        for first, last, gain, out in (
            (0, QRANK, gq, query_gain_out),
            (QRANK, LATENT, gl, latent_gain_out),
        ):
            source = latent_ref[:, first:last]
            grad = sums[:, first:last]
            inverse = lax.rsqrt(jnp.mean(source * source, axis=1, keepdims=True) + EPSILON)
            out[...] = jnp.sum(grad * source * inverse, axis=0, keepdims=True)
            scaled = grad * gain[...]
            inner = jnp.mean(scaled * source, axis=1, keepdims=True)
            parts.append(inverse * scaled - source * (inverse * inverse * inverse * inner))
        rope = turn_lanes(sums[:, LATENT:], cos_t[...], lower_t[...], upper_t[...], -1.0)
        parts.append(pltpu.roll(rope, LANES - NOPE, 1))
        latent_grad = jnp.concatenate(parts, axis=1)
        low = latent_grad.astype(BF16)
        down_grad = transposed_times(low, normed_ref[...]).astype(BF16)
        if paired:
            stage_q[...] = down_grad[:QRANK]
            gains = [
                jnp.concatenate(
                    [
                        query_gain_out[:, i * query_rows : (i + 1) * query_rows],
                        latent_gain_out[:, i * KVRANK // shards : (i + 1) * KVRANK // shards],
                        jnp.zeros((1, width - LANES), F32),
                    ],
                    axis=1,
                )
                for i in range(shards)
            ]
            first = LATENT + ROPE - QRANK
            low_part = jnp.concatenate(
                [
                    down_grad[QRANK : LATENT + ROPE].astype(F32),
                    jnp.concatenate(gains, axis=0),
                    jnp.zeros((LOW_ROWS - first - shards, width), F32),
                ],
                axis=0,
            ).astype(BF16)
            stage_low[...] = transposed_times(pick_ref[...], low_part).astype(BF16)
            for index, out in enumerate(outs):
                place = shard_place(where_ref, index, n_ctx)
                out[:query_rows, :] = stage_q[
                    pl.ds(pl.multiple_of(place * query_rows, SUBLANES), query_rows), :
                ]
                out[query_rows:, :] = stage_low[
                    pl.ds(pl.multiple_of(place * low_rows, SUBLANES), low_rows), :
                ]
        else:
            outs[0][...] = down_grad
        row_inner = jnp.sum(latent_grad * latent_ref[...], axis=1, keepdims=True)
        normed_grad = product(low, joined_ref[...])
        source = act_ref[...].astype(F32)
        inverse = inverse_ref[...]
        gain_out[...] = jnp.sum(normed_grad * source * inverse, axis=0, keepdims=True)
        input_out[...] = (
            middle_ref[...]
            + inverse * (normed_grad * gain_ref[...])
            - source * (inverse * inverse * row_inner / full_width)
        )

    if paired:
        outputs = [(shape((query_rows + low_rows, width)), VMEM)] * shards
    else:
        outputs = [(shape((LAT_COLS, width)), VMEM)]
    arrays = (mine, other, latent, gain_query, gain_latent) + tables
    arrays += (normed, joined, activations, inverse_one, gain_one, middle_grad, pick)
    return run_kernel(
        body,
        [(where, SMEM)] + [(a, VMEM) for a in arrays],
        [
            (shape((rows, width), F32), VMEM),
            (shape((1, QRANK), F32), VMEM),
            (shape((1, KVRANK), F32), VMEM),
            (shape((1, width), F32), VMEM),
        ]
        + outputs,
        [
            pltpu.VMEM((rows, LAT_COLS), F32),
            pltpu.VMEM((QRANK, width), BF16),
            pltpu.VMEM((low_in, width), BF16),
        ],
        4 * rows * width * LAT_COLS,
        12 << 20,
        "input_backward",
        waits=waits,
    )


def pick_matrix(columns, rows_each, valid):
    matrix = np.zeros((LOW_ROWS, columns), np.float32)
    for row in range(KVRANK + ROPE):
        matrix[row, row // valid * rows_each + row % valid] = 1.0
    for shard in range(columns // rows_each if rows_each > valid else 0):
        matrix[KVRANK + ROPE + shard, shard * rows_each + valid] = 1.0
    return jnp.asarray(matrix, BF16)


def per_device(
    activations,
    attn_gain,
    query_down,
    latent_down,
    query_gain,
    latent_gain,
    query_up,
    latent_up,
    attn_output,
    ffn_gain,
    ffn_gate,
    ffn_up,
    ffn_down,
    out_grad,
):
    n_fsdp = lax.axis_size("fsdp")
    n_ctx = lax.axis_size("ctx")
    n_tp = lax.axis_size("tp")
    shards = n_fsdp * n_ctx
    paired = n_fsdp == 2 and shards == 2 * n_tp
    rows, width = activations.shape
    full_width = width * n_tp
    fsdp_index = lax.axis_index("fsdp").astype(jnp.int32)
    ctx_index = lax.axis_index("ctx").astype(jnp.int32)
    tp_index = lax.axis_index("tp").astype(jnp.int32)
    shard_index = fsdp_index * n_ctx + ctx_index
    where = jnp.stack([fsdp_index, ctx_index, tp_index, tp_index % 2])
    local_heads = query_up.shape[1] // (NOPE + ROPE)
    hidden = ffn_gate.shape[1] // n_ctx
    columns = round_up(3 * hidden, LANES)
    q_shard = query_down.shape[1]
    low_shard = latent_down.shape[1]
    both_axes = ("fsdp", "ctx")

    def spread_shards(own):
        pieces = spread_ctx(own)
        return pieces + [swap(piece, "fsdp", 1) for piece in pieces]

    def fold_shards(parts):
        return [
            (parts[k].astype(F32) + swap(parts[n_ctx + k], "fsdp", 1).astype(F32)).astype(BF16)
            for k in range(n_ctx)
        ]

    def gather_rows(value):
        return lax.all_gather(value, both_axes, axis=0, tiled=True)

    def scatter_rows(value):
        return lax.psum_scatter(value, both_axes, scatter_dimension=0, tiled=True).astype(F32)

    def spread_sequence(own):
        return [spread_tp(block) for block in spread_ctx(own)]

    inputs = activations.astype(F32)
    gain_one = attn_gain.astype(F32)
    row_sums = total_tp(jnp.sum(inputs * inputs, axis=1))
    inverse_one = lax.rsqrt(row_sums / full_width + EPSILON)
    gain_two = ffn_gain.astype(F32)
    gains_two = spread_tp(jnp.broadcast_to(gain_two[None, :], (8, width)))
    normed_low = (inputs * inverse_one[:, None] * gain_one).astype(BF16)

    query_pad = jnp.pad(
        query_up.reshape(query_up.shape[0], local_heads, NOPE + ROPE),
        ((0, 0), (0, 0), (0, LANES - NOPE - ROPE)),
    ).reshape(query_up.shape[0], local_heads * LANES)
    if paired:
        low_rows = round_up(low_shard, SUBLANES)
        pick = pick_matrix(shards * low_rows, low_rows, low_shard)
        down_own = jnp.concatenate(
            [
                query_down.T,
                latent_down.T,
                jnp.pad(
                    jnp.concatenate([query_gain, latent_gain])[None, :],
                    ((0, low_rows - low_shard - 1), (0, width - LANES)),
                ),
            ]
        )
        query_pieces = low_pieces = spread_shards(down_own)
        first_low = q_shard
        ups = spread_shards(jnp.concatenate([query_pad, latent_up])) + spread_shards(attn_output.T)
    else:
        low_rows = low_shard
        pick = pick_matrix(LOW_ROWS, KVRANK + ROPE, KVRANK + ROPE)
        query_pieces = [gather_rows(query_down.T)]
        low_pieces = [
            jnp.pad(gather_rows(latent_down.T), ((0, LOW_ROWS - KVRANK - ROPE), (0, 0)))
        ]
        first_low = 0
        ups = [gather_rows(query_pad), gather_rows(latent_up), gather_rows(attn_output.T)]

    parts = 2 if paired else 1
    chunks = cut_hidden(where, ffn_gate, ffn_up, ffn_down, parts=parts)
    if paired:
        sent = {(part, k): chunks[n_ctx * part + k] for part in range(parts) for k in range(1, n_ctx)}
        order = [[(part, k) for k in group] for part in range(parts) for group in ((2, 1), (3,))]
        _, got = in_turn(sent, order, lambda key, value: swap(value, "ctx", key[1]))
        got.update({(part, 0): chunks[n_ctx * part] for part in range(parts)})
        order = [[(part, 0)] for part in range(parts)]
        order += [[(part, k)] for part in range(parts) for k in range(1, n_ctx)]
        got, crossed = in_turn(got, order, lambda key, value: swap(value, "fsdp", 1))
        weights = []
        for part in range(parts):
            weights += [got[part, k] for k in range(n_ctx)]
            weights += [crossed[part, k] for k in range(n_ctx)]
    else:
        stack = jnp.stack(exchange_ctx(chunks))
        stack = jnp.stack(
            [
                lax.dynamic_index_in_dim(stack, ctx_index ^ k, 0, keepdims=False)
                for k in range(n_ctx)
            ]
        )
        weights = [lax.all_gather(stack, "fsdp", axis=0).reshape(full_width, columns)]

    upstream = out_grad.astype(F32)
    branches = spread_sequence((RESID * upstream).astype(BF16))

    keep, send, joined, gain_query, gain_latent = latent_products(
        where,
        normed_low,
        pick,
        query_pieces,
        low_pieces,
        q_shard,
        low_rows,
        first_low,
        n_ctx,
        paired,
        waits=list(chunks[:1]) + ups[1:2],
    )
    if not paired:
        gains = jnp.zeros((QRANK + KVRANK,), F32)
        gains = lax.dynamic_update_slice(
            gains, query_gain.astype(F32), (shard_index * query_gain.shape[0],)
        )
        gains = lax.dynamic_update_slice(
            gains, latent_gain.astype(F32), (QRANK + shard_index * latent_gain.shape[0],)
        )
        gains = lax.psum(gains, both_axes)
        gain_query = gains[None, :QRANK]
        gain_latent = gains[None, QRANK:]
    mine, other = fold_halves(keep, send)
    query_pos = ctx_index * rows + jnp.arange(rows, dtype=jnp.int32)
    tables = lane_tables(*rotary_tables(query_pos.astype(F32)))
    latent, query_low, payload = latent_norms(where, mine, other, gain_query, gain_latent, tables)
    payloads = spread_ctx(payload)

    attended, queries_low, pairs_low, lse = attention_forward(
        where, query_low, payloads, ups, tables, local_heads, n_ctx
    )

    def fold_tp(keep, send):
        got = swap(send, "tp", 1)
        far = (keep[1].astype(F32) + got[1].astype(F32)).astype(BF16)
        near = keep[0].astype(F32) + got[0].astype(F32)
        return near + swap(far, "tp", 2).astype(F32)

    keep, send = output_products(where, attended, ups, full_width, n_ctx)
    middle = inputs + RESID * fold_tp(keep, send)

    tokens = spread_sequence((middle * gain_two).astype(BF16))
    pairs_grad, active, keep, send, inverse_two = feed_forward(
        where, tokens, branches, weights, gains_two, hidden, n_ctx
    )
    inverse_two = inverse_two[:, :1]

    def fold_sequence(keep, send):
        got = swap(send, "tp", 1)
        totals = []
        for block in reversed(range(n_ctx)):
            here = slice(block * rows, (block + 1) * rows)
            far = (keep[1, here].astype(F32) + got[1, here].astype(F32)).astype(BF16)
            near = keep[0, here].astype(F32) + got[0, here].astype(F32)
            totals.append(near + swap(far, "tp", 2).astype(F32))
        return sum_ctx(totals[::-1])

    second_grad = fold_sequence(keep, send)
    scaled_two = second_grad * gain_two
    grad_gain_two = jnp.sum(second_grad * middle, axis=0)
    inner_two = lax.psum(jnp.sum(scaled_two * middle, axis=1), "tp") / full_width
    middle_grad = upstream + scaled_two - middle * (inverse_two * inverse_two * inner_two[:, None])
    branch = spread_tp((RESID * middle_grad).astype(BF16))

    result = middle + RESID * fold_sequence(
        *feed_forward_result(where, active, weights, hidden, n_ctx)
    )
    grads = functools.partial(
        feed_forward_grads, where, tokens, branches, pairs_grad, active, hidden, columns, shards, n_ctx
    )
    if paired:
        sent, kept = grads(1), grads(0)
        moved = [swap(sent[k], "fsdp", 1) for k in reversed(range(n_ctx))][::-1]
        sums = [
            (kept[k].astype(F32) + moved[k].astype(F32)).astype(BF16) for k in range(n_ctx)
        ]
    else:
        total = grads(None)[0].reshape(n_fsdp, n_ctx, full_width // shards, columns)
        total = lax.psum_scatter(total, "fsdp", scatter_dimension=0, tiled=False)
        sums = [
            lax.dynamic_index_in_dim(total, ctx_index ^ k, 0, keepdims=False) for k in range(n_ctx)
        ]
    sent = {k: sums[k] for k in range(1, n_ctx)}
    _, got = in_turn(sent, ((3, 1), (2,)), lambda key, value: swap(value, "ctx", key))
    hidden_sums = [sums[0]] + [got[k] for k in range(1, n_ctx)]

    query_grad, pair_grad, query_sum, kv_keep, kv_1, kv_2, kv_3 = attention_backward(
        where, queries_low, pairs_low, lse, payloads, ups, branch, tables, n_ctx
    )
    kv_total = sum_ctx([kv_keep, kv_1, kv_2, kv_3])
    both = jnp.concatenate([query_sum, kv_total], axis=1).reshape(2, rows // 2, LAT_COLS)
    mine, other = fold_halves(
        lax.dynamic_index_in_dim(both, tp_index % 2, 0, keepdims=False),
        lax.dynamic_index_in_dim(both, 1 - tp_index % 2, 0, keepdims=False),
    )
    out_parts = output_grads(where, attended, branch, shards, n_ctx, paired)
    up_parts = up_grads(
        where, query_low, query_grad, payloads, pair_grad, shards, n_ctx, paired
    )
    if paired:
        out_sums = fold_shards(out_parts)
        up_sums = fold_shards(up_parts)
    input_grad, grad_query_gain, grad_latent_gain, grad_gain_one, *down_parts = input_backward(
        where,
        mine,
        other,
        latent,
        gain_query,
        gain_latent,
        tables,
        normed_low,
        joined,
        activations,
        inverse_one[:, None],
        gain_one[None, :],
        middle_grad,
        pick,
        q_shard,
        low_rows,
        shards,
        n_ctx,
        paired,
    )
    grad_gate, grad_up, grad_down = join_hidden(where, hidden_sums, hidden)
    if paired:
        grad_out = sum_ctx(out_sums)
        grad_ups = sum_ctx(up_sums)
        grad_query_up = grad_ups[: query_up.shape[0]]
        grad_latent_up = grad_ups[query_up.shape[0] :]
        grad_downs = sum_ctx(fold_shards(down_parts))
        grad_query_down = grad_downs[:q_shard]
        grad_latent_down = grad_downs[q_shard : q_shard + low_shard]
    else:
        grad_out = scatter_rows(out_parts[0])
        grad_query_up, grad_latent_up = scatter_rows(up_parts[0]), scatter_rows(up_parts[1])
        grad_query_down = scatter_rows(down_parts[0][:QRANK])
        grad_latent_down = scatter_rows(down_parts[0][QRANK : LATENT + ROPE])
    grad_query_up = grad_query_up.reshape(query_up.shape[0], local_heads, LANES)
    grad_query_up = grad_query_up[:, :, : NOPE + ROPE].reshape(query_up.shape)

    gain_sums = lax.psum(jnp.concatenate([grad_gain_one[0], grad_gain_two]), both_axes)
    if paired:
        gain_row = grad_downs[q_shard + low_shard]
        gain_query_sum = gain_row[:q_shard]
        gain_latent_sum = gain_row[q_shard : q_shard + latent_gain.shape[0]]
    else:
        gain_query_sum = scatter_rows(grad_query_gain[0])
        gain_latent_sum = scatter_rows(grad_latent_gain[0])
    return (
        result.astype(BF16),
        input_grad,
        gain_sums[:width],
        grad_query_down.T,
        grad_latent_down.T,
        gain_query_sum,
        gain_latent_sum,
        grad_query_up,
        grad_latent_up,
        grad_out.T,
        gain_sums[width : 2 * width],
        grad_gate,
        grad_up,
        grad_down.T,
    )


def solution(mesh):
    tokens = P(("fsdp", "ctx"), "tp")
    by_columns = P("tp", ("fsdp", "ctx"))
    by_rows = P(("fsdp", "ctx"), "tp")
    latent_vector = P(("fsdp", "ctx"))
    feature_vector = P("tp")
    weights = (
        feature_vector,
        by_columns,
        by_columns,
        latent_vector,
        latent_vector,
        by_rows,
        by_rows,
        by_columns,
        feature_vector,
        by_rows,
        by_rows,
        by_columns,
    )
    return jax.shard_map(
        per_device,
        mesh=mesh,
        in_specs=(tokens,) + weights + (tokens,),
        out_specs=(tokens, tokens) + weights,
        check_vma=False,
    )
```

profile of v0, /device:TPU:0, one launch (start us, length us, event | category | flops | bytes accessed | tf_op | source)
XLA Modules:
  0.0 612.4 jit_solution(3957956576152126802)
XLA Ops:
  14.8 4.5 cut_hidden.1
  27.9 4.7 collective-permute-done.6.refs_8_
  35.8 5.1 latent_products.1
  42.5 10.5 %collective-permute-done.66.refs_1_ = bf16[160,1280]{1,0:T(8,128)(2,1)S(1)} collective-permute-done((bf16[160,1280]{1,0:T(8,128)(2,1)S(1)}, bf16[160,1280]{1,0:T(8,128)(2,1)S(1)}, u32[]{:S(2)}, u32[]{:S(2)}) %collective-permute-start.66) | collective-permute-done | bytes 409632 | tf_op jit(solution)/shard_map/ppermute | solution.py:81
  56.3 7.5 %collective-permute-done.64.refs_1_ = bf16[160,1280]{1,0:T(8,128)(2,1)S(1)} collective-permute-done((bf16[160,1280]{1,0:T(8,128)(2,1)}, bf16[160,1280]{1,0:T(8,128)(2,1)S(1)}, u32[]{:S(2)}, u32[]{:S(2)}) %collective-permute-start.64) | collective-permute-done | bytes 409632 | tf_op jit(solution)/shard_map/ppermute | solution.py:81
  68.7 8.5 %collective-permute-done.16.refs_11_.refs_4_.refs_13_ = bf16[128,1280]{1,0:T(8,128)(2,1)S(1)} collective-permute-done((bf16[128,1280]{1,0:T(8,128)(2,1)S(1)}, bf16[128,1280]{1,0:T(8,128)(2,1)S(1)}, u32[]{:S(2)}, u32[]{:S(2)}) %collective-permute-start.16) | collective-permute-done | bytes 327712 | tf_op jit(solution)/shard_map/ppermute | solution.py:81
  78.7 6.5 %collective-permute-done.22.refs_18_.refs_11_.refs_20_ = bf16[320,640]{1,0:T(8,128)(2,1)} collective-permute-done((bf16[320,640]{1,0:T(8,128)(2,1)S(1)}, bf16[320,640]{1,0:T(8,128)(2,1)}, u32[]{:S(2)}, u32[]{:S(2)}) %collective-permute-start.22) | collective-permute-done | bytes 409632 | tf_op jit(solution)/shard_map/ppermute | solution.py:81
  85.7 9.0 %collective-permute-done.23.refs_19_.refs_12_.refs_21_ = bf16[320,640]{1,0:T(8,128)(2,1)} collective-permute-done((bf16[320,640]{1,0:T(8,128)(2,1)S(1)}, bf16[320,640]{1,0:T(8,128)(2,1)}, u32[]{:S(2)}, u32[]{:S(2)}) %collective-permute-start.23) | collective-permute-done | bytes 409632 | tf_op jit(solution)/shard_map/ppermute | solution.py:81
  97.0 7.7 %collective-permute-done.17.refs_12_.refs_5_.refs_14_ = bf16[128,1280]{1,0:T(8,128)(2,1)} collective-permute-done((bf16[128,1280]{1,0:T(8,128)(2,1)}, bf16[128,1280]{1,0:T(8,128)(2,1)}, u32[]{:S(2)}, u32[]{:S(2)}) %collective-permute-start.17) | collective-permute-done | bytes 327712 | tf_op jit(solution)/shard_map/ppermute | solution.py:81
  111.1 4.0 collective-permute-start.14
  115.2 10.3 %collective-permute-done.24.refs_20_.refs_13_.refs_22_ = bf16[320,640]{1,0:T(8,128)(2,1)} collective-permute-done((bf16[320,640]{1,0:T(8,128)(2,1)}, bf16[320,640]{1,0:T(8,128)(2,1)}, u32[]{:S(2)}, u32[]{:S(2)}) %collective-permute-start.24) | collective-permute-done | bytes 409632 | tf_op jit(solution)/shard_map/ppermute | solution.py:81
  132.8 5.2 collective-permute-done.27.refs_23_.refs_16_.refs_25_
  139.6 10.6 %collective-permute-done.21.refs_16_.refs_9_.refs_18_ = bf16[128,1280]{1,0:T(8,128)(2,1)} collective-permute-done((bf16[128,1280]{1,0:T(8,128)(2,1)}, bf16[128,1280]{1,0:T(8,128)(2,1)}, u32[]{:S(2)}, u32[]{:S(2)}) %collective-permute-start.21) | collective-permute-done | bytes 327712 | tf_op jit(solution)/shard_map/ppermute | solution.py:81
  157.9 15.3 %attention_forward.1 = (bf16[256,640]{1,0:T(8,128)(2,1)}, bf16[256,1280]{1,0:T(8,128)(2,1)}, bf16[1024,1280]{1,0:T(8,128)(2,1)}, f32[5,8,256]{2,1,0:T(8,128)}) custom-call(s32[4]{0:T(128)} %pad_add_fusion.refs_0_, bf16[256,768]{1,0:T(8,128)(2,1)} %get-tuple-element.118.refs_1_, f32[256,128]{1,0:T(8,128)} %get-tuple-element.282.refs_5_.refs_2_.refs_4_.refs_6_, ...), custom_call_target="tpu_custom_call" | custom-call | flops 2516582400 | bytes 12582912 | tf_op jit(solution)/shard_map/attention_forward/pallas_call | solution.py:195
  173.4 5.9 output_products.1
  183.9 11.8 %collective-permute-done.49.refs_21_.refs_23_ = bf16[256,640]{1,0:T(8,128)(2,1)} collective-permute-done((bf16[256,640]{1,0:T(8,128)(2,1)S(1)}, bf16[256,640]{1,0:T(8,128)(2,1)}, u32[]{:S(2)}, u32[]{:S(2)}) %collective-permute-start.49) | collective-permute-done | bytes 327712 | tf_op jit(solution)/shard_map/ppermute | solution.py:81
  201.9 5.7 collective-permute-done.57.refs_29_.refs_31_
  216.1 7.0 %collective-permute-done.59.refs_31_.refs_33_ = bf16[256,640]{1,0:T(8,128)(2,1)} collective-permute-done((bf16[256,640]{1,0:T(8,128)(2,1)}, bf16[256,640]{1,0:T(8,128)(2,1)}, u32[]{:S(2)}, u32[]{:S(2)}) %collective-permute-start.59) | collective-permute-done | bytes 327712 | tf_op jit(solution)/shard_map/ppermute | solution.py:81
  223.1 5.6 collective-permute-done.30
  235.7 13.9 %collective-permute-done.38.refs_9_.refs_11_ = bf16[256,640]{1,0:T(8,128)(2,1)S(1)} collective-permute-done((bf16[256,640]{1,0:T(8,128)(2,1)S(1)}, bf16[256,640]{1,0:T(8,128)(2,1)S(1)}, u32[]{:S(2)}, u32[]{:S(2)}) %collective-permute-start.38) | collective-permute-done | bytes 327712 | tf_op jit(solution)/shard_map/ppermute | solution.py:81
  252.2 6.7 %collective-permute-done.42.refs_13_.refs_15_ = bf16[256,640]{1,0:T(8,128)(2,1)S(1)} collective-permute-done((bf16[256,640]{1,0:T(8,128)(2,1)S(1)}, bf16[256,640]{1,0:T(8,128)(2,1)S(1)}, u32[]{:S(2)}, u32[]{:S(2)}) %collective-permute-start.42) | collective-permute-done | bytes 327712 | tf_op jit(solution)/shard_map/ppermute | solution.py:81
  260.8 7.0 %collective-permute-done.40.refs_11_.refs_13_ = bf16[256,640]{1,0:T(8,128)(2,1)S(1)} collective-permute-done((bf16[256,640]{1,0:T(8,128)(2,1)S(1)}, bf16[256,640]{1,0:T(8,128)(2,1)S(1)}, u32[]{:S(2)}, u32[]{:S(2)}) %collective-permute-start.40) | collective-permute-done | bytes 327712 | tf_op jit(solution)/shard_map/ppermute | solution.py:81
  267.8 6.2 %collective-permute-done.44.refs_15_.refs_17_ = bf16[256,640]{1,0:T(8,128)(2,1)S(1)} collective-permute-done((bf16[256,640]{1,0:T(8,128)(2,1)S(1)}, bf16[256,640]{1,0:T(8,128)(2,1)S(1)}, u32[]{:S(2)}, u32[]{:S(2)}) %collective-permute-start.44) | collective-permute-done | bytes 327712 | tf_op jit(solution)/shard_map/ppermute | solution.py:81
  276.3 25.9 %feed_forward.1 = (bf16[1024,896]{1,0:T(8,128)(2,1)}, bf16[1024,512]{1,0:T(8,128)(2,1)}, bf16[2,1024,640]{2,1,0:T(8,128)(2,1)}, bf16[2,1024,640]{2,1,0:T(8,128)(2,1)}, f32[256,128]{1,0:T(8,128)}) custom-call(s32[4]{0:T(128)} %pad_add_fusion.refs_0_, bf16[256,640]{1,0:T(8,128)(2,1)} %copy-done.3, bf16[256,640]{1,0:T(8,128)(2,1)} %copy-done.26, ...), custom_call_target="tpu_custom_call" | custom-call | flops 10485760000 | bytes 29360128 | tf_op jit(solution)/shard_map/feed_forward/pallas_call | solution.py:195
  302.4 9.9 %feed_forward_result.1 = (bf16[2,1024,640]{2,1,0:T(8,128)(2,1)}, bf16[2,1024,640]{2,1,0:T(8,128)(2,1)}) custom-call(s32[4]{0:T(128)} %pad_add_fusion.refs_0_, bf16[1024,512]{1,0:T(8,128)(2,1)} %get-tuple-element.153.refs_1_.refs_2_, bf16[160,1280]{1,0:T(8,128)(2,1)} %get-tuple-element.113.refs_11_.refs_37_.refs_2_, ...), custom_call_target="tpu_custom_call" | custom-call | flops 2097152000 | bytes 10485760 | tf_op jit(solution)/shard_map/feed_forward_result/pallas_call | solution.py:195
  317.1 12.5 %feed_forward_grads.3 = (bf16[320,1280]{1,0:T(8,128)(2,1)}, bf16[320,1280]{1,0:T(8,128)(2,1)}, bf16[320,1280]{1,0:T(8,128)(2,1)}, bf16[320,1280]{1,0:T(8,128)(2,1)}) custom-call(s32[4]{0:T(128)} %pad_add_fusion.refs_0_, bf16[1024,896]{1,0:T(8,128)(2,1)} %get-tuple-element.197.refs_1_, bf16[1024,512]{1,0:T(8,128)(2,1)} %get-tuple-element.153.refs_1_.refs_2_, ...), custom_call_target="tpu_custom_call" | custom-call | flops 3145728000 | bytes 18874368 | tf_op jit(solution)/shard_map/feed_forward_grads/pallas_call | solution.py:195
  339.9 11.9 %feed_forward_grads.2 = (bf16[320,1280]{1,0:T(8,128)(2,1)}, bf16[320,1280]{1,0:T(8,128)(2,1)}, bf16[320,1280]{1,0:T(8,128)(2,1)}, bf16[320,1280]{1,0:T(8,128)(2,1)}) custom-call(s32[4]{0:T(128)} %pad_add_fusion.refs_0_, bf16[1024,896]{1,0:T(8,128)(2,1)} %get-tuple-element.197.refs_1_, bf16[1024,512]{1,0:T(8,128)(2,1)} %get-tuple-element.153.refs_1_.refs_2_, ...), custom_call_target="tpu_custom_call" | custom-call | flops 3145728000 | bytes 18874368 | tf_op jit(solution)/shard_map/feed_forward_grads/pallas_call | solution.py:195
  369.1 10.0 %collective-permute-done.84 = bf16[256,640]{1,0:T(8,128)(2,1)S(1)} collective-permute-done((bf16[256,640]{1,0:T(8,128)(2,1)S(1)}, bf16[256,640]{1,0:T(8,128)(2,1)S(1)}, u32[]{:S(2)}, u32[]{:S(2)}) %collective-permute-start.84) | collective-permute-done | bytes 327712 | tf_op jit(solution)/shard_map/ppermute | solution.py:81
  383.1 5.4 collective-permute-start.85
  390.6 6.0 psum.14
  407.4 17.8 %collective-permute-start.129 = (bf16[320,1280]{1,0:T(8,128)(2,1)}, bf16[320,1280]{1,0:T(8,128)(2,1)S(1)}, u32[]{:S(2)}, u32[]{:S(2)}) collective-permute-start(bf16[320,1280]{1,0:T(8,128)(2,1)} %add_convert_fusion), channel_id=1, source_target_pairs={{0,4},{4,0},{8,12},{12,8},{1,5},{5,1},{9,13},{13,9},{2,6},{6,2},{1... | collective-permute-start | bytes 2457608 | tf_op jit(solution)/shard_map/ppermute | solution.py:81
  430.0 6.2 %collective-permute-done.129.refs_2_ = bf16[320,1280]{1,0:T(8,128)(2,1)S(1)} collective-permute-done((bf16[320,1280]{1,0:T(8,128)(2,1)}, bf16[320,1280]{1,0:T(8,128)(2,1)S(1)}, u32[]{:S(2)}, u32[]{:S(2)}) %collective-permute-start.129) | collective-permute-done | bytes 819232 | tf_op jit(solution)/shard_map/ppermute | solution.py:81
  437.2 4.2 collective-permute-start.130
  441.3 22.9 %attention_backward.1 = (bf16[256,1280]{1,0:T(8,128)(2,1)}, bf16[1024,1280]{1,0:T(8,128)(2,1)}, f32[256,768]{1,0:T(8,128)}, f32[256,384]{1,0:T(8,128)}, bf16[256...) custom-call(s32[4]{0:T(128)} %pad_add_fusion.refs_0_, ...), custom_call_target="tpu_custom_call" | custom-call | flops 3355443200 | bytes 25165824 | tf_op jit(solution)/shard_map/attention_backward/pallas_call | solution.py:195
  466.6 6.2 %up_grads.1 = (bf16[128,1280]{1,0:T(8,128)(2,1)}, bf16[128,1280]{1,0:T(8,128)(2,1)}, bf16[128,1280]{1,0:T(8,128)(2,1)}, bf16[128,1280]{1,0:T(8,128)(2,1)}, bf16[...) custom-call(s32[4]{0:T(128)} %pad_add_fusion.refs_0_, ...), custom_call_target="tpu_custom_call" | custom-call | flops 1174405120 | bytes 10485760 | tf_op jit(solution)/shard_map/up_grads/pallas_call | solution.py:195
  476.7 5.9 join_hidden.1
  484.9 5.2 output_grads.1
  492.5 7.8 %collective-permute-done.99 = bf16[256,384]{1,0:T(8,128)(2,1)S(1)} collective-permute-done((bf16[256,384]{1,0:T(8,128)(2,1)S(1)}, bf16[256,384]{1,0:T(8,128)(2,1)S(1)}, u32[]{:S(2)}, u32[]{:S(2)}) %collective-permute-start.99) | collective-permute-done | bytes 196640 | tf_op jit(solution)/shard_map/ppermute | solution.py:81
  502.0 14.3 %collective-permute-done.121 = bf16[320,640]{1,0:T(8,128)(2,1)S(1)} collective-permute-done((bf16[320,640]{1,0:T(8,128)(2,1)}, bf16[320,640]{1,0:T(8,128)(2,1)S(1)}, u32[]{:S(2)}, u32[]{:S(2)}) %collective-permute-start.121) | collective-permute-done | bytes 409632 | tf_op jit(solution)/shard_map/ppermute | solution.py:81
  517.8 6.2 %collective-permute-done.118 = bf16[320,640]{1,0:T(8,128)(2,1)S(1)} collective-permute-done((bf16[320,640]{1,0:T(8,128)(2,1)}, bf16[320,640]{1,0:T(8,128)(2,1)S(1)}, u32[]{:S(2)}, u32[]{:S(2)}) %collective-permute-start.118) | collective-permute-done | bytes 409632 | tf_op jit(solution)/shard_map/ppermute | solution.py:81
  531.7 6.3 %collective-permute-start.101 = (bf16[128,1152]{1,0:T(8,128)(2,1)S(1)}, bf16[128,1152]{1,0:T(8,128)(2,1)S(1)}, u32[]{:S(2)}, u32[]{:S(2)}) collective-permute-start(bf16[128,1152]{1,0:T(8,128)(2,1)S(1)} %fusion.21), channel_id=1, source_target_pairs={{0,2},{1,3},{2,0},{3,1},{4,6},{5,7},{6,4},{7,5},{8,10},{9,11},{10,... | collective-permute-start | bytes 884744 | tf_op jit(solution)/shard_map/ppermute | solution.py:81
  538.2 4.6 collective-permute-done.101
  548.3 7.7 %collective-permute-done.116 = bf16[128,1280]{1,0:T(8,128)(2,1)S(1)} collective-permute-done((bf16[128,1280]{1,0:T(8,128)(2,1)S(1)}, bf16[128,1280]{1,0:T(8,128)(2,1)S(1)}, u32[]{:S(2)}, u32[]{:S(2)}) %collective-permute-start.116) | collective-permute-done | bytes 327712 | tf_op jit(solution)/shard_map/ppermute | solution.py:81
  559.0 6.1 input_backward.1
  567.1 4.0 collective-permute-done.123
  575.4 19.8 %psum.15 = f32[1280]{0:T(1024)S(1)} all-reduce(f32[1280]{0:T(1024)S(1)} %pad_maximum_fusion.3), channel_id=1, replica_groups=mesh['fsdp'=2,'ctx'=4,'tp'=4] {'fsdp','ctx'}, use_global_device_ids=true, to_apply=%region_4.5 | all-reduce | flops 1280 | bytes 10240 | tf_op jit(solution)/shard_map/psum | solution.py:1377
  597.5 4.7 collective-permute-done.108
  604.1 5.6 collective-permute-done.109
  (531 shorter events, 194.0 us)
Async XLA Ops:
  41.7 22.2 %collective-permute-start.64 = (bf16[160,1280]{1,0:T(8,128)(2,1)}, bf16[160,1280]{1,0:T(8,128)(2,1)S(1)}, u32[]{:S(2)}, u32[]{:S(2)}) collective-permute-start(bf16[160,1280]{1,0:T(8,128)(2,1)} %get-tuple-element.124), channel_id=1, source_target_pairs={{0,8},{4,12},{8,0},{12,4},{1,9},{5,13},{9,1},{13,5},{2,10},{6,14},... | collective-permute-start | bytes 1228808 | tf_op jit(solution)/shard_map/ppermute | solution.py:81
  42.0 23.3 %collective-permute-start.65 = (bf16[160,1280]{1,0:T(8,128)(2,1)}, bf16[160,1280]{1,0:T(8,128)(2,1)S(1)}, u32[]{:S(2)}, u32[]{:S(2)}) collective-permute-start(bf16[160,1280]{1,0:T(8,128)(2,1)} %get-tuple-element.125), channel_id=1, source_target_pairs={{0,4},{4,0},{8,12},{12,8},{1,5},{5,1},{9,13},{13,9},{2,6},{6,2},{1... | collective-permute-start | bytes 1228808 | tf_op jit(solution)/shard_map/ppermute | solution.py:81
  56.0 21.2 %collective-permute-start.16 = (bf16[128,1280]{1,0:T(8,128)(2,1)S(1)}, bf16[128,1280]{1,0:T(8,128)(2,1)S(1)}, u32[]{:S(2)}, u32[]{:S(2)}) collective-permute-start(bf16[128,1280]{1,0:T(8,128)(2,1)S(1)} %pad_maximum_fusion.1.refs_9_.refs_2_.refs_11_), channel_id=1, source_target_pairs={{0,8},{4,12},{8,0},{12,4},{1,9},{5,13},{9,1},{13,5},{2,10},{6,14},... | collective-permute-start | bytes 983048 | tf_op jit(solution)/shard_map/ppermute | solution.py:81
  66.1 28.6 %collective-permute-start.23 = (bf16[320,640]{1,0:T(8,128)(2,1)S(1)}, bf16[320,640]{1,0:T(8,128)(2,1)}, u32[]{:S(2)}, u32[]{:S(2)}) collective-permute-start(bf16[320,640]{1,0:T(8,128)(2,1)S(1)} %bitcast.117), channel_id=1, source_target_pairs={{0,8},{4,12},{8,0},{12,4},{1,9},{5,13},{9,1},{13,5},{2,10},{6,14},... | collective-permute-start | bytes 1228808 | tf_op jit(solution)/shard_map/ppermute | solution.py:81
  68.2 27.3 %collective-permute-start.25 = (bf16[320,640]{1,0:T(8,128)(2,1)S(1)}, bf16[320,640]{1,0:T(8,128)(2,1)S(1)}, u32[]{:S(2)}, u32[]{:S(2)}) collective-permute-start(bf16[320,640]{1,0:T(8,128)(2,1)S(1)} %bitcast.118), channel_id=1, source_target_pairs={{0,16},{16,0},{1,17},{17,1},{2,18},{18,2},{3,19},{19,3},{4,20},{20... | collective-permute-start | bytes 1228808 | tf_op jit(solution)/shard_map/ppermute | solution.py:81
  77.2 27.9 %collective-permute-start.68 = (bf16[160,1280]{1,0:T(8,128)(2,1)}, bf16[160,1280]{1,0:T(8,128)(2,1)}, u32[]{:S(2)}, u32[]{:S(2)}) collective-permute-start(bf16[160,1280]{1,0:T(8,128)(2,1)} %get-tuple-element.129.refs_38_.refs_3_), channel_id=1, source_target_pairs={{0,16},{16,0},{1,17},{17,1},{2,18},{18,2},{3,19},{19,3},{4,20},{20... | collective-permute-start | bytes 1228808 | tf_op jit(solution)/shard_map/ppermute | solution.py:81
  78.7 28.2 %collective-permute-start.12 = (f32[128,1152]{1,0:T(8,128)S(1)}, f32[128,1152]{1,0:T(8,128)S(1)}, u32[]{:S(2)}, u32[]{:S(2)}) collective-permute-start(f32[128,1152]{1,0:T(8,128)S(1)} %convert_add_fusion.4.refs_1_), channel_id=1, source_target_pairs={{0,1},{1,0},{2,3},{3,2},{4,5},{5,4},{6,7},{7,6},{8,9},{9,8},{10,11... | collective-permute-start | bytes 1769480 | tf_op jit(solution)/shard_map/ppermute | solution.py:81
  104.7 22.8 %collective-permute-start.69 = (bf16[160,1280]{1,0:T(8,128)(2,1)}, bf16[160,1280]{1,0:T(8,128)(2,1)S(1)}, u32[]{:S(2)}, u32[]{:S(2)}) collective-permute-start(bf16[160,1280]{1,0:T(8,128)(2,1)} %get-tuple-element.134), channel_id=1, source_target_pairs={{0,12},{4,8},{8,4},{12,0},{1,13},{5,9},{9,5},{13,1},{2,14},{6,10},... | collective-permute-start | bytes 1228808 | tf_op jit(solution)/shard_map/ppermute | solution.py:81
  105.1 21.9 %collective-permute-start.26 = (bf16[320,640]{1,0:T(8,128)(2,1)}, bf16[320,640]{1,0:T(8,128)(2,1)S(1)}, u32[]{:S(2)}, u32[]{:S(2)}) collective-permute-start(bf16[320,640]{1,0:T(8,128)(2,1)} %collective-permute-done.22.refs_18_.refs_11_.refs_20_), channel_id=1, source_target_pairs={{0,16},{16,0},{1,17},{17,1},{2,18},{18,2},{3,19},{19,3},{4,20},{20... | collective-permute-start | bytes 1228808 | tf_op jit(solution)/shard_map/ppermute | solution.py:81
  106.9 22.1 %collective-permute-start.70 = (bf16[160,1280]{1,0:T(8,128)(2,1)}, bf16[160,1280]{1,0:T(8,128)(2,1)S(1)}, u32[]{:S(2)}, u32[]{:S(2)}) collective-permute-start(bf16[160,1280]{1,0:T(8,128)(2,1)} %get-tuple-element.131.refs_39_.refs_4_), channel_id=1, source_target_pairs={{0,16},{16,0},{1,17},{17,1},{2,18},{18,2},{3,19},{19,3},{4,20},{20... | collective-permute-start | bytes 1228808 | tf_op jit(solution)/shard_map/ppermute | solution.py:81
  111.1 21.6 %collective-permute-start.14 = (bf16[256,384]{1,0:T(8,128)(2,1)}, bf16[256,384]{1,0:T(8,128)(2,1)S(1)}, u32[]{:S(2)}, u32[]{:S(2)}) collective-permute-start(bf16[256,384]{1,0:T(8,128)(2,1)} %get-tuple-element.119.refs_5_.refs_7_.refs_4_), channel_id=1, source_target_pairs={{0,8},{4,12},{8,0},{12,4},{1,9},{5,13},{9,1},{13,5},{2,10},{6,14},... | collective-permute-start | bytes 589832 | tf_op jit(solution)/shard_map/ppermute | solution.py:81
  127.0 26.1 %collective-permute-start.28 = (bf16[320,640]{1,0:T(8,128)(2,1)}, bf16[320,640]{1,0:T(8,128)(2,1)S(1)}, u32[]{:S(2)}, u32[]{:S(2)}) collective-permute-start(bf16[320,640]{1,0:T(8,128)(2,1)} %collective-permute-done.24.refs_20_.refs_13_.refs_22_), channel_id=1, source_target_pairs={{0,16},{16,0},{1,17},{17,1},{2,18},{18,2},{3,19},{19,3},{4,20},{20... | collective-permute-start | bytes 1228808 | tf_op jit(solution)/shard_map/ppermute | solution.py:81
  127.5 22.7 %collective-permute-start.21 = (bf16[128,1280]{1,0:T(8,128)(2,1)}, bf16[128,1280]{1,0:T(8,128)(2,1)}, u32[]{:S(2)}, u32[]{:S(2)}) collective-permute-start(bf16[128,1280]{1,0:T(8,128)(2,1)} %collective-permute-done.17.refs_12_.refs_5_.refs_14_), channel_id=1, source_target_pairs={{0,16},{16,0},{1,17},{17,1},{2,18},{18,2},{3,19},{19,3},{4,20},{20... | collective-permute-start | bytes 983048 | tf_op jit(solution)/shard_map/ppermute | solution.py:81
  129.0 25.9 %collective-permute-start.13 = (bf16[256,384]{1,0:T(8,128)(2,1)}, bf16[256,384]{1,0:T(8,128)(2,1)}, u32[]{:S(2)}, u32[]{:S(2)}) collective-permute-start(bf16[256,384]{1,0:T(8,128)(2,1)} %get-tuple-element.119.refs_5_.refs_7_.refs_4_), channel_id=1, source_target_pairs={{0,4},{4,0},{8,12},{12,8},{1,5},{5,1},{9,13},{13,9},{2,6},{6,2},{1... | collective-permute-start | bytes 589832 | tf_op jit(solution)/shard_map/ppermute | solution.py:81
  132.7 24.9 %collective-permute-start.15 = (bf16[256,384]{1,0:T(8,128)(2,1)S(1)}, bf16[256,384]{1,0:T(8,128)(2,1)}, u32[]{:S(2)}, u32[]{:S(2)}) collective-permute-start(bf16[256,384]{1,0:T(8,128)(2,1)S(1)} %collective-permute-done.14.refs_7_.refs_9_.refs_6_), channel_id=1, source_target_pairs={{0,4},{4,0},{8,12},{12,8},{1,5},{5,1},{9,13},{13,9},{2,6},{6,2},{1... | collective-permute-start | bytes 589832 | tf_op jit(solution)/shard_map/ppermute | solution.py:81
  138.1 35.2 %collective-permute-start.62 = (f32[8,640]{1,0:T(8,128)S(1)}, f32[8,640]{1,0:T(8,128)S(1)}, u32[]{:S(2)}, u32[]{:S(2)}) collective-permute-start(f32[8,640]{1,0:T(8,128)S(1)} %broadcast_in_dim.41.refs_33_), channel_id=1, source_target_pairs={{0,2},{1,3},{2,0},{3,1},{4,6},{5,7},{6,4},{7,5},{8,10},{9,11},{10,... | collective-permute-start | bytes 61448 | tf_op jit(solution)/shard_map/ppermute | solution.py:81
  150.2 29.6 %collective-permute-start.47 = (bf16[256,640]{1,0:T(8,128)(2,1)S(1)}, bf16[256,640]{1,0:T(8,128)(2,1)S(1)}, u32[]{:S(2)}, u32[]{:S(2)}) collective-permute-start(bf16[256,640]{1,0:T(8,128)(2,1)S(1)} %fusion.refs_17_.refs_19_), channel_id=1, source_target_pairs={{0,2},{1,3},{2,0},{3,1},{4,6},{5,7},{6,4},{7,5},{8,10},{9,11},{10,... | collective-permute-start | bytes 983048 | tf_op jit(solution)/shard_map/ppermute | solution.py:81
  153.1 26.8 %collective-permute-start.71 = (bf16[160,1280]{1,0:T(8,128)(2,1)}, bf16[160,1280]{1,0:T(8,128)(2,1)S(1)}, u32[]{:S(2)}, u32[]{:S(2)}) collective-permute-start(bf16[160,1280]{1,0:T(8,128)(2,1)} %get-tuple-element.141), channel_id=1, source_target_pairs={{0,8},{4,12},{8,0},{12,4},{1,9},{5,13},{9,1},{13,5},{2,10},{6,14},... | collective-permute-start | bytes 1228808 | tf_op jit(solution)/shard_map/ppermute | solution.py:81
  154.8 25.1 %collective-permute-start.72 = (bf16[160,1280]{1,0:T(8,128)(2,1)}, bf16[160,1280]{1,0:T(8,128)(2,1)S(1)}, u32[]{:S(2)}, u32[]{:S(2)}) collective-permute-start(bf16[160,1280]{1,0:T(8,128)(2,1)} %get-tuple-element.142), channel_id=1, source_target_pairs={{0,4},{4,0},{8,12},{12,8},{1,5},{5,1},{9,13},{13,9},{2,6},{6,2},{1... | collective-permute-start | bytes 1228808 | tf_op jit(solution)/shard_map/ppermute | solution.py:81
  157.6 22.8 %collective-permute-start.73 = (bf16[160,1280]{1,0:T(8,128)(2,1)}, bf16[160,1280]{1,0:T(8,128)(2,1)}, u32[]{:S(2)}, u32[]{:S(2)}) collective-permute-start(bf16[160,1280]{1,0:T(8,128)(2,1)} %get-tuple-element.136.refs_40_.refs_5_), channel_id=1, source_target_pairs={{0,16},{16,0},{1,17},{17,1},{2,18},{18,2},{3,19},{19,3},{4,20},{20... | collective-permute-start | bytes 1228808 | tf_op jit(solution)/shard_map/ppermute | solution.py:81
  182.1 26.5 %collective-permute-start.74 = (bf16[160,1280]{1,0:T(8,128)(2,1)}, bf16[160,1280]{1,0:T(8,128)(2,1)S(1)}, u32[]{:S(2)}, u32[]{:S(2)}) collective-permute-start(bf16[160,1280]{1,0:T(8,128)(2,1)} %get-tuple-element.145.refs_46_.refs_11_), channel_id=1, source_target_pairs={{0,16},{16,0},{1,17},{17,1},{2,18},{18,2},{3,19},{19,3},{4,20},{20... | collective-permute-start | bytes 1228808 | tf_op jit(solution)/shard_map/ppermute | solution.py:81
  329.7 32.4 %collective-permute-start.126 = (bf16[320,1280]{1,0:T(8,128)(2,1)}, bf16[320,1280]{1,0:T(8,128)(2,1)S(1)}, u32[]{:S(2)}, u32[]{:S(2)}) collective-permute-start(bf16[320,1280]{1,0:T(8,128)(2,1)} %get-tuple-element.203), channel_id=1, source_target_pairs={{0,16},{16,0},{1,17},{17,1},{2,18},{18,2},{3,19},{19,3},{4,20},{20... | collective-permute-start | bytes 2457608 | tf_op jit(solution)/shard_map/ppermute | solution.py:81
  331.5 27.0 %collective-permute-start.90 = (bf16[256,640]{1,0:T(8,128)(2,1)}, bf16[256,640]{1,0:T(8,128)(2,1)S(1)}, u32[]{:S(2)}, u32[]{:S(2)}) collective-permute-start(bf16[256,640]{1,0:T(8,128)(2,1)} %get-tuple-element.263), channel_id=1, source_target_pairs={{0,2},{1,3},{2,0},{3,1},{4,6},{5,7},{6,4},{7,5},{8,10},{9,11},{10,... | collective-permute-start | bytes 983048 | tf_op jit(solution)/shard_map/ppermute | solution.py:81
  337.9 22.9 %collective-permute-start.92 = (bf16[256,640]{1,0:T(8,128)(2,1)S(1)}, bf16[256,640]{1,0:T(8,128)(2,1)S(1)}, u32[]{:S(2)}, u32[]{:S(2)}) collective-permute-start(bf16[256,640]{1,0:T(8,128)(2,1)S(1)} %get-tuple-element.266), channel_id=1, source_target_pairs={{0,4},{4,0},{8,12},{12,8},{1,5},{5,1},{9,13},{13,9},{2,6},{6,2},{1... | collective-permute-start | bytes 983048 | tf_op jit(solution)/shard_map/ppermute | solution.py:81
  351.8 30.1 %collective-permute-start.87 = (bf16[256,640]{1,0:T(8,128)(2,1)S(1)}, bf16[256,640]{1,0:T(8,128)(2,1)S(1)}, u32[]{:S(2)}, u32[]{:S(2)}) collective-permute-start(bf16[256,640]{1,0:T(8,128)(2,1)S(1)} %get-tuple-element.261), channel_id=1, source_target_pairs={{0,2},{1,3},{2,0},{3,1},{4,6},{5,7},{6,4},{7,5},{8,10},{9,11},{10,... | collective-permute-start | bytes 983048 | tf_op jit(solution)/shard_map/ppermute | solution.py:81
  358.6 24.5 %collective-permute-start.89 = (bf16[256,640]{1,0:T(8,128)(2,1)S(1)}, bf16[256,640]{1,0:T(8,128)(2,1)S(1)}, u32[]{:S(2)}, u32[]{:S(2)}) collective-permute-start(bf16[256,640]{1,0:T(8,128)(2,1)S(1)} %get-tuple-element.265), channel_id=1, source_target_pairs={{0,4},{4,0},{8,12},{12,8},{1,5},{5,1},{9,13},{13,9},{2,6},{6,2},{1... | collective-permute-start | bytes 983048 | tf_op jit(solution)/shard_map/ppermute | solution.py:81
  362.1 21.1 %collective-permute-start.93 = (bf16[256,640]{1,0:T(8,128)(2,1)S(1)}, bf16[256,640]{1,0:T(8,128)(2,1)S(1)}, u32[]{:S(2)}, u32[]{:S(2)}) collective-permute-start(bf16[256,640]{1,0:T(8,128)(2,1)S(1)} %fusion.7), channel_id=1, source_target_pairs={{0,8},{4,12},{8,0},{12,4},{1,9},{5,13},{9,1},{13,5},{2,10},{6,14},... | collective-permute-start | bytes 983048 | tf_op jit(solution)/shard_map/ppermute | solution.py:81
  368.7 58.5 %collective-permute-start.125 = (bf16[320,1280]{1,0:T(8,128)(2,1)}, bf16[320,1280]{1,0:T(8,128)(2,1)}, u32[]{:S(2)}, u32[]{:S(2)}) collective-permute-start(bf16[320,1280]{1,0:T(8,128)(2,1)} %get-tuple-element.201), channel_id=1, source_target_pairs={{0,16},{16,0},{1,17},{17,1},{2,18},{18,2},{3,19},{19,3},{4,20},{20... | collective-permute-start | bytes 2457608 | tf_op jit(solution)/shard_map/ppermute | solution.py:81
  379.1 26.0 %collective-permute-start.128 = (bf16[320,1280]{1,0:T(8,128)(2,1)}, bf16[320,1280]{1,0:T(8,128)(2,1)}, u32[]{:S(2)}, u32[]{:S(2)}) collective-permute-start(bf16[320,1280]{1,0:T(8,128)(2,1)} %get-tuple-element.205), channel_id=1, source_target_pairs={{0,16},{16,0},{1,17},{17,1},{2,18},{18,2},{3,19},{19,3},{4,20},{20... | collective-permute-start | bytes 2457608 | tf_op jit(solution)/shard_map/ppermute | solution.py:81
  396.9 33.1 %collective-permute-start.127 = (bf16[320,1280]{1,0:T(8,128)(2,1)}, bf16[320,1280]{1,0:T(8,128)(2,1)S(1)}, u32[]{:S(2)}, u32[]{:S(2)}) collective-permute-start(bf16[320,1280]{1,0:T(8,128)(2,1)} %add_convert_fusion.1), channel_id=1, source_target_pairs={{0,12},{4,8},{8,4},{12,0},{1,13},{5,9},{9,5},{13,1},{2,14},{6,10},... | collective-permute-start | bytes 2457608 | tf_op jit(solution)/shard_map/ppermute | solution.py:81
  402.7 24.5 %collective-permute-start.95 = (bf16[256,640]{1,0:T(8,128)(2,1)S(1)}, bf16[256,640]{1,0:T(8,128)(2,1)S(1)}, u32[]{:S(2)}, u32[]{:S(2)}) collective-permute-start(bf16[256,640]{1,0:T(8,128)(2,1)S(1)} %get-tuple-element.256.refs_27_.refs_2_), channel_id=1, source_target_pairs={{0,2},{1,3},{2,0},{3,1},{4,6},{5,7},{6,4},{7,5},{8,10},{9,11},{10,... | collective-permute-start | bytes 983048 | tf_op jit(solution)/shard_map/ppermute | solution.py:81
  407.4 28.8 %collective-permute-start.129 = (bf16[320,1280]{1,0:T(8,128)(2,1)}, bf16[320,1280]{1,0:T(8,128)(2,1)S(1)}, u32[]{:S(2)}, u32[]{:S(2)}) collective-permute-start(bf16[320,1280]{1,0:T(8,128)(2,1)} %add_convert_fusion), channel_id=1, source_target_pairs={{0,4},{4,0},{8,12},{12,8},{1,5},{5,1},{9,13},{13,9},{2,6},{6,2},{1... | collective-permute-start | bytes 2457608 | tf_op jit(solution)/shard_map/ppermute | solution.py:81
  426.6 47.0 %collective-permute-start.124 = (bf16[320,1280]{1,0:T(8,128)(2,1)}, bf16[320,1280]{1,0:T(8,128)(2,1)}, u32[]{:S(2)}, u32[]{:S(2)}) collective-permute-start(bf16[320,1280]{1,0:T(8,128)(2,1)} %get-tuple-element.199), channel_id=1, source_target_pairs={{0,16},{16,0},{1,17},{17,1},{2,18},{18,2},{3,19},{19,3},{4,20},{20... | collective-permute-start | bytes 2457608 | tf_op jit(solution)/shard_map/ppermute | solution.py:81
  437.2 38.7 %collective-permute-start.130 = (bf16[320,1280]{1,0:T(8,128)(2,1)}, bf16[320,1280]{1,0:T(8,128)(2,1)S(1)}, u32[]{:S(2)}, u32[]{:S(2)}) collective-permute-start(bf16[320,1280]{1,0:T(8,128)(2,1)} %get-tuple-element.207), channel_id=1, source_target_pairs={{0,8},{4,12},{8,0},{12,4},{1,9},{5,13},{9,1},{13,5},{2,10},{6,14},... | collective-permute-start | bytes 2457608 | tf_op jit(solution)/shard_map/ppermute | solution.py:81
  464.2 25.8 %collective-permute-start.98 = (bf16[256,384]{1,0:T(8,128)(2,1)}, bf16[256,384]{1,0:T(8,128)(2,1)S(1)}, u32[]{:S(2)}, u32[]{:S(2)}) collective-permute-start(bf16[256,384]{1,0:T(8,128)(2,1)} %get-tuple-element.166), channel_id=1, source_target_pairs={{0,4},{4,0},{8,12},{12,8},{1,5},{5,1},{9,13},{13,9},{2,6},{6,2},{1... | collective-permute-start | bytes 589832 | tf_op jit(solution)/shard_map/ppermute | solution.py:81
  482.8 44.2 %collective-permute-start.113 = (bf16[128,1280]{1,0:T(8,128)(2,1)S(1)}, bf16[128,1280]{1,0:T(8,128)(2,1)S(1)}, u32[]{:S(2)}, u32[]{:S(2)}) collective-permute-start(bf16[128,1280]{1,0:T(8,128)(2,1)S(1)} %copy-done.95), channel_id=1, source_target_pairs={{0,16},{16,0},{1,17},{17,1},{2,18},{18,2},{3,19},{19,3},{4,20},{20... | collective-permute-start | bytes 983048 | tf_op jit(solution)/shard_map/ppermute | solution.py:81
  490.1 55.2 %collective-permute-start.110 = (bf16[128,1280]{1,0:T(8,128)(2,1)S(1)}, bf16[128,1280]{1,0:T(8,128)(2,1)S(1)}, u32[]{:S(2)}, u32[]{:S(2)}) collective-permute-start(bf16[128,1280]{1,0:T(8,128)(2,1)S(1)} %copy-done.93), channel_id=1, source_target_pairs={{0,16},{16,0},{1,17},{17,1},{2,18},{18,2},{3,19},{19,3},{4,20},{20... | collective-permute-start | bytes 983048 | tf_op jit(solution)/shard_map/ppermute | solution.py:81
  491.8 24.5 %collective-permute-start.121 = (bf16[320,640]{1,0:T(8,128)(2,1)}, bf16[320,640]{1,0:T(8,128)(2,1)S(1)}, u32[]{:S(2)}, u32[]{:S(2)}) collective-permute-start(bf16[320,640]{1,0:T(8,128)(2,1)} %get-tuple-element.196), channel_id=1, source_target_pairs={{0,16},{16,0},{1,17},{17,1},{2,18},{18,2},{3,19},{19,3},{4,20},{20... | collective-permute-start | bytes 1228808 | tf_op jit(solution)/shard_map/ppermute | solution.py:81
  500.3 23.7 %collective-permute-start.118 = (bf16[320,640]{1,0:T(8,128)(2,1)}, bf16[320,640]{1,0:T(8,128)(2,1)S(1)}, u32[]{:S(2)}, u32[]{:S(2)}) collective-permute-start(bf16[320,640]{1,0:T(8,128)(2,1)} %get-tuple-element.192), channel_id=1, source_target_pairs={{0,16},{16,0},{1,17},{17,1},{2,18},{18,2},{3,19},{19,3},{4,20},{20... | collective-permute-start | bytes 1228808 | tf_op jit(solution)/shard_map/ppermute | solution.py:81
  501.2 25.3 %collective-permute-start.100 = (f32[128,1152]{1,0:T(8,128)S(1)}, f32[128,1152]{1,0:T(8,128)S(1)}, u32[]{:S(2)}, u32[]{:S(2)}) collective-permute-start(f32[128,1152]{1,0:T(8,128)S(1)} %dynamic-slice_bitcast_fusion), channel_id=1, source_target_pairs={{0,1},{1,0},{2,3},{3,2},{4,5},{5,4},{6,7},{7,6},{8,9},{9,8},{10,11... | collective-permute-start | bytes 1769480 | tf_op jit(solution)/shard_map/ppermute | solution.py:81
  516.3 26.5 %collective-permute-start.120 = (bf16[320,640]{1,0:T(8,128)(2,1)S(1)}, bf16[320,640]{1,0:T(8,128)(2,1)S(1)}, u32[]{:S(2)}, u32[]{:S(2)}) collective-permute-start(bf16[320,640]{1,0:T(8,128)(2,1)S(1)} %copy-done.92), channel_id=1, source_target_pairs={{0,16},{16,0},{1,17},{17,1},{2,18},{18,2},{3,19},{19,3},{4,20},{20... | collective-permute-start | bytes 1228808 | tf_op jit(solution)/shard_map/ppermute | solution.py:81
  542.8 23.5 %collective-permute-start.117 = (bf16[320,640]{1,0:T(8,128)(2,1)}, bf16[320,640]{1,0:T(8,128)(2,1)S(1)}, u32[]{:S(2)}, u32[]{:S(2)}) collective-permute-start(bf16[320,640]{1,0:T(8,128)(2,1)} %get-tuple-element.190), channel_id=1, source_target_pairs={{0,16},{16,0},{1,17},{17,1},{2,18},{18,2},{3,19},{19,3},{4,20},{20... | collective-permute-start | bytes 1228808 | tf_op jit(solution)/shard_map/ppermute | solution.py:81
  545.2 21.9 %collective-permute-start.119 = (bf16[320,640]{1,0:T(8,128)(2,1)}, bf16[320,640]{1,0:T(8,128)(2,1)S(1)}, u32[]{:S(2)}, u32[]{:S(2)}) collective-permute-start(bf16[320,640]{1,0:T(8,128)(2,1)} %add_convert_fusion.7), channel_id=1, source_target_pairs={{0,4},{4,0},{8,12},{12,8},{1,5},{5,1},{9,13},{13,9},{2,6},{6,2},{1... | collective-permute-start | bytes 1228808 | tf_op jit(solution)/shard_map/ppermute | solution.py:81
  547.2 23.9 %collective-permute-start.123 = (bf16[320,640]{1,0:T(8,128)(2,1)}, bf16[320,640]{1,0:T(8,128)(2,1)S(1)}, u32[]{:S(2)}, u32[]{:S(2)}) collective-permute-start(bf16[320,640]{1,0:T(8,128)(2,1)} %add_convert_fusion.4), channel_id=1, source_target_pairs={{0,8},{4,12},{8,0},{12,4},{1,9},{5,13},{9,1},{13,5},{2,10},{6,14},... | collective-permute-start | bytes 1228808 | tf_op jit(solution)/shard_map/ppermute | solution.py:81
  565.2 30.0 %collective-permute-start.107 = (bf16[144,640]{1,0:T(8,128)(2,1)}, bf16[144,640]{1,0:T(8,128)(2,1)S(1)}, u32[]{:S(2)}, u32[]{:S(2)}) collective-permute-start(bf16[144,640]{1,0:T(8,128)(2,1)} %get-tuple-element.178), channel_id=1, source_target_pairs={{0,16},{16,0},{1,17},{17,1},{2,18},{18,2},{3,19},{19,3},{4,20},{20... | collective-permute-start | bytes 552968 | tf_op jit(solution)/shard_map/ppermute | solution.py:81
  572.3 25.2 %collective-permute-start.106 = (bf16[144,640]{1,0:T(8,128)(2,1)S(1)}, bf16[144,640]{1,0:T(8,128)(2,1)S(1)}, u32[]{:S(2)}, u32[]{:S(2)}) collective-permute-start(bf16[144,640]{1,0:T(8,128)(2,1)S(1)} %copy-done.99), channel_id=1, source_target_pairs={{0,16},{16,0},{1,17},{17,1},{2,18},{18,2},{3,19},{19,3},{4,20},{20... | collective-permute-start | bytes 552968 | tf_op jit(solution)/shard_map/ppermute | solution.py:81
  573.3 22.0 %collective-permute-start.104 = (bf16[144,640]{1,0:T(8,128)(2,1)S(1)}, bf16[144,640]{1,0:T(8,128)(2,1)S(1)}, u32[]{:S(2)}, u32[]{:S(2)}) collective-permute-start(bf16[144,640]{1,0:T(8,128)(2,1)S(1)} %copy-done.100), channel_id=1, source_target_pairs={{0,16},{16,0},{1,17},{17,1},{2,18},{18,2},{3,19},{19,3},{4,20},{20... | collective-permute-start | bytes 552968 | tf_op jit(solution)/shard_map/ppermute | solution.py:81
  574.3 28.6 %collective-permute-start.103 = (bf16[144,640]{1,0:T(8,128)(2,1)S(1)}, bf16[144,640]{1,0:T(8,128)(2,1)S(1)}, u32[]{:S(2)}, u32[]{:S(2)}) collective-permute-start(bf16[144,640]{1,0:T(8,128)(2,1)S(1)} %copy-done.98), channel_id=1, source_target_pairs={{0,16},{16,0},{1,17},{17,1},{2,18},{18,2},{3,19},{19,3},{4,20},{20... | collective-permute-start | bytes 552968 | tf_op jit(solution)/shard_map/ppermute | solution.py:81
  (187 other events, 2877.8 us)
where the time goes:
time: 619 us; the launch traced here: 612 us
  waiting for transfers between devices  246 us (40%)
  starting transfers between devices  142 us (23%)
  Pallas kernels  140 us (23%)
  other arithmetic  39.1 us (6%)
  blocking collectives  25.8 us (4%)
  local copies, waits for them, and re-layouts  16.9 us (3%)
    ppermute x131, waiting for transfers between devices, swap(): return lax.ppermute(value, axis, [(i, i ^ distance) for i in range(size)])  246 us
    ppermute x131, starting transfers between devices, swap(): return lax.ppermute(value, axis, [(i, i ^ distance) for i in range(size)])  142 us
    pallas_call x14, Pallas kernels, run_kernel(): pl.pallas_call(used, grid=grid if grid is not None else (), in_specs=[spe...  140 us
    psum x1, blocking collectives, per_device(): lax.psum(jnp.concatenate([grad_gain_one[0], grad_gain_two]), both_axes)  19.8 us
  transfers between devices with their start and end apart: 131, of which 44 were waited for; matrix products, arithmetic and copies ran while one was open for 7% of the time, Pallas kernels for 18%

commit v1 on v0

--- a/solution.py
+++ b/solution.py
@@ -836,7 +836,15 @@
         normed, branch, stage, sems = rest[-4:]
         copies = sequence_copies(where_ref, token_refs, normed, rows, width, sems, 0)
         copies += sequence_copies(where_ref, branch_refs, branch, rows, width, sems, count)
-        at_once(sum(copies, []))
+        if distance is not None:
+            for place in range(4):
+
+                @pl.when(((where_ref[2] ^ place) >> 1) == (where_ref[0] ^ distance))
+                def _():
+                    at_once([group[place] for group in copies])
+
+        else:
+            at_once(sum(copies, []))
         if distance is None:
             for place in range(4):
                 here = slice(place * width, (place + 1) * width)
@@ -1320,8 +1328,18 @@
     _, got = in_turn(sent, ((3, 1), (2,)), lambda key, value: swap(value, "ctx", key))
     hidden_sums = [sums[0]] + [got[k] for k in range(1, n_ctx)]
 
+    out_parts = output_grads(where, attended, branch, shards, n_ctx, paired)
     query_grad, pair_grad, query_sum, kv_keep, kv_1, kv_2, kv_3 = attention_backward(
-        where, queries_low, pairs_low, lse, payloads, ups, branch, tables, n_ctx
+        where,
+        queries_low,
+        pairs_low,
+        lse,
+        payloads,
+        ups,
+        branch,
+        tables,
+        n_ctx,
+        waits=out_parts[:1],
     )
     kv_total = sum_ctx([kv_keep, kv_1, kv_2, kv_3])
     both = jnp.concatenate([query_sum, kv_total], axis=1).reshape(2, rows // 2, LAT_COLS)
@@ -1329,7 +1347,6 @@
         lax.dynamic_index_in_dim(both, tp_index % 2, 0, keepdims=False),
         lax.dynamic_index_in_dim(both, 1 - tp_index % 2, 0, keepdims=False),
     )
-    out_parts = output_grads(where, attended, branch, shards, n_ctx, paired)
     up_parts = up_grads(
         where, query_low, query_grad, payloads, pair_grad, shards, n_ctx, paired
     )

time: 619 us -> 622 us (level)
  waiting for transfers between devices: 246 us -> 255 us
    ppermute x131, waiting for transfers between devices: 246 us -> 255 us  [swap(): return lax.ppermute(value, axis, [(i, i ^ distance) for i in range(size)])]
  transfers between devices with their start and end apart: 131 -> 131, of which waited for: 44 -> 47; matrix products, arithmetic and copies ran while one was open for 7% -> 7% of each run, Pallas kernels for 18% -> 17%
where the time goes in v1:
time: 622 us; the launch traced here: 615 us
  waiting for transfers between devices  255 us (41%)
  Pallas kernels  139 us (22%)
  starting transfers between devices  136 us (22%)
  other arithmetic  39.1 us (6%)
  blocking collectives  26.5 us (4%)
  local copies, waits for them, and re-layouts  16.3 us (3%)
    ppermute x131, waiting for transfers between devices, swap(): return lax.ppermute(value, axis, [(i, i ^ distance) for i in range(size)])  255 us
    pallas_call x14, Pallas kernels, run_kernel(): pl.pallas_call(used, grid=grid if grid is not None else (), in_specs=[spe...  139 us
    ppermute x131, starting transfers between devices, swap(): return lax.ppermute(value, axis, [(i, i ^ distance) for i in range(size)])  136 us
    psum x1, blocking collectives, per_device(): lax.psum(jnp.concatenate([grad_gain_one[0], grad_gain_two]), both_axes)  20.5 us
  transfers between devices with their start and end apart: 131, of which 47 were waited for; matrix products, arithmetic and copies ran while one was open for 7% of the time, Pallas kernels for 17%

profile of v1, /device:TPU:0, one launch (start us, length us, event | category | flops | bytes accessed | tf_op | source)
XLA Modules:
  0.0 614.5 jit_solution(15736046806956168906)
XLA Ops:
  14.9 4.5 cut_hidden.1
  27.9 4.7 collective-permute-done.6.refs_8_
  35.9 5.1 latent_products.1
  42.5 10.5 %collective-permute-done.66.refs_1_ = bf16[160,1280]{1,0:T(8,128)(2,1)S(1)} collective-permute-done((bf16[160,1280]{1,0:T(8,128)(2,1)S(1)}, bf16[160,1280]{1,0:T(8,128)(2,1)S(1)}, u32[]{:S(2)}, u32[]{:S(2)}) %collective-permute-start.66) | collective-permute-done | bytes 409632 | tf_op jit(solution)/shard_map/ppermute | solution.py:81
  56.4 7.5 %collective-permute-done.64.refs_1_ = bf16[160,1280]{1,0:T(8,128)(2,1)S(1)} collective-permute-done((bf16[160,1280]{1,0:T(8,128)(2,1)}, bf16[160,1280]{1,0:T(8,128)(2,1)S(1)}, u32[]{:S(2)}, u32[]{:S(2)}) %collective-permute-start.64) | collective-permute-done | bytes 409632 | tf_op jit(solution)/shard_map/ppermute | solution.py:81
  68.7 8.5 %collective-permute-done.16.refs_11_.refs_4_.refs_13_ = bf16[128,1280]{1,0:T(8,128)(2,1)S(1)} collective-permute-done((bf16[128,1280]{1,0:T(8,128)(2,1)S(1)}, bf16[128,1280]{1,0:T(8,128)(2,1)S(1)}, u32[]{:S(2)}, u32[]{:S(2)}) %collective-permute-start.16) | collective-permute-done | bytes 327712 | tf_op jit(solution)/shard_map/ppermute | solution.py:81
  78.7 6.5 %collective-permute-done.22.refs_18_.refs_11_.refs_20_ = bf16[320,640]{1,0:T(8,128)(2,1)} collective-permute-done((bf16[320,640]{1,0:T(8,128)(2,1)S(1)}, bf16[320,640]{1,0:T(8,128)(2,1)}, u32[]{:S(2)}, u32[]{:S(2)}) %collective-permute-start.22) | collective-permute-done | bytes 409632 | tf_op jit(solution)/shard_map/ppermute | solution.py:81
  85.8 9.0 %collective-permute-done.23.refs_19_.refs_12_.refs_21_ = bf16[320,640]{1,0:T(8,128)(2,1)} collective-permute-done((bf16[320,640]{1,0:T(8,128)(2,1)S(1)}, bf16[320,640]{1,0:T(8,128)(2,1)}, u32[]{:S(2)}, u32[]{:S(2)}) %collective-permute-start.23) | collective-permute-done | bytes 409632 | tf_op jit(solution)/shard_map/ppermute | solution.py:81
  97.0 7.7 %collective-permute-done.17.refs_12_.refs_5_.refs_14_ = bf16[128,1280]{1,0:T(8,128)(2,1)} collective-permute-done((bf16[128,1280]{1,0:T(8,128)(2,1)}, bf16[128,1280]{1,0:T(8,128)(2,1)}, u32[]{:S(2)}, u32[]{:S(2)}) %collective-permute-start.17) | collective-permute-done | bytes 327712 | tf_op jit(solution)/shard_map/ppermute | solution.py:81
  111.2 4.0 collective-permute-start.14
  115.2 10.3 %collective-permute-done.24.refs_20_.refs_13_.refs_22_ = bf16[320,640]{1,0:T(8,128)(2,1)} collective-permute-done((bf16[320,640]{1,0:T(8,128)(2,1)}, bf16[320,640]{1,0:T(8,128)(2,1)}, u32[]{:S(2)}, u32[]{:S(2)}) %collective-permute-start.24) | collective-permute-done | bytes 409632 | tf_op jit(solution)/shard_map/ppermute | solution.py:81
  132.9 5.2 collective-permute-done.27.refs_23_.refs_16_.refs_25_
  139.6 10.6 %collective-permute-done.21.refs_16_.refs_9_.refs_18_ = bf16[128,1280]{1,0:T(8,128)(2,1)} collective-permute-done((bf16[128,1280]{1,0:T(8,128)(2,1)}, bf16[128,1280]{1,0:T(8,128)(2,1)}, u32[]{:S(2)}, u32[]{:S(2)}) %collective-permute-start.21) | collective-permute-done | bytes 327712 | tf_op jit(solution)/shard_map/ppermute | solution.py:81
  157.8 15.0 %attention_forward.1 = (bf16[256,640]{1,0:T(8,128)(2,1)}, bf16[256,1280]{1,0:T(8,128)(2,1)}, bf16[1024,1280]{1,0:T(8,128)(2,1)}, f32[5,8,256]{2,1,0:T(8,128)}) custom-call(s32[4]{0:T(128)} %pad_add_fusion.refs_0_, bf16[256,768]{1,0:T(8,128)(2,1)} %get-tuple-element.118.refs_1_, f32[256,128]{1,0:T(8,128)} %get-tuple-element.282.refs_5_.refs_2_.refs_4_.refs_6_, ...), custom_call_target="tpu_custom_call" | custom-call | flops 2516582400 | bytes 12582912 | tf_op jit(solution)/shard_map/attention_forward/pallas_call | solution.py:195
  172.9 5.9 output_products.1
  183.5 11.8 %collective-permute-done.49.refs_21_.refs_23_ = bf16[256,640]{1,0:T(8,128)(2,1)} collective-permute-done((bf16[256,640]{1,0:T(8,128)(2,1)S(1)}, bf16[256,640]{1,0:T(8,128)(2,1)}, u32[]{:S(2)}, u32[]{:S(2)}) %collective-permute-start.49) | collective-permute-done | bytes 327712 | tf_op jit(solution)/shard_map/ppermute | solution.py:81
  201.5 5.7 collective-permute-done.57.refs_29_.refs_31_
  215.7 7.0 %collective-permute-done.59.refs_31_.refs_33_ = bf16[256,640]{1,0:T(8,128)(2,1)} collective-permute-done((bf16[256,640]{1,0:T(8,128)(2,1)}, bf16[256,640]{1,0:T(8,128)(2,1)}, u32[]{:S(2)}, u32[]{:S(2)}) %collective-permute-start.59) | collective-permute-done | bytes 327712 | tf_op jit(solution)/shard_map/ppermute | solution.py:81
  222.7 5.6 collective-permute-done.30
  235.3 13.9 %collective-permute-done.38.refs_9_.refs_11_ = bf16[256,640]{1,0:T(8,128)(2,1)S(1)} collective-permute-done((bf16[256,640]{1,0:T(8,128)(2,1)S(1)}, bf16[256,640]{1,0:T(8,128)(2,1)S(1)}, u32[]{:S(2)}, u32[]{:S(2)}) %collective-permute-start.38) | collective-permute-done | bytes 327712 | tf_op jit(solution)/shard_map/ppermute | solution.py:81
  251.8 6.7 %collective-permute-done.42.refs_13_.refs_15_ = bf16[256,640]{1,0:T(8,128)(2,1)S(1)} collective-permute-done((bf16[256,640]{1,0:T(8,128)(2,1)S(1)}, bf16[256,640]{1,0:T(8,128)(2,1)S(1)}, u32[]{:S(2)}, u32[]{:S(2)}) %collective-permute-start.42) | collective-permute-done | bytes 327712 | tf_op jit(solution)/shard_map/ppermute | solution.py:81
  260.3 7.0 %collective-permute-done.40.refs_11_.refs_13_ = bf16[256,640]{1,0:T(8,128)(2,1)S(1)} collective-permute-done((bf16[256,640]{1,0:T(8,128)(2,1)S(1)}, bf16[256,640]{1,0:T(8,128)(2,1)S(1)}, u32[]{:S(2)}, u32[]{:S(2)}) %collective-permute-start.40) | collective-permute-done | bytes 327712 | tf_op jit(solution)/shard_map/ppermute | solution.py:81
  267.3 6.2 %collective-permute-done.44.refs_15_.refs_17_ = bf16[256,640]{1,0:T(8,128)(2,1)S(1)} collective-permute-done((bf16[256,640]{1,0:T(8,128)(2,1)S(1)}, bf16[256,640]{1,0:T(8,128)(2,1)S(1)}, u32[]{:S(2)}, u32[]{:S(2)}) %collective-permute-start.44) | collective-permute-done | bytes 327712 | tf_op jit(solution)/shard_map/ppermute | solution.py:81
  275.9 26.1 %feed_forward.1 = (bf16[1024,896]{1,0:T(8,128)(2,1)}, bf16[1024,512]{1,0:T(8,128)(2,1)}, bf16[2,1024,640]{2,1,0:T(8,128)(2,1)}, bf16[2,1024,640]{2,1,0:T(8,128)(2,1)}, f32[256,128]{1,0:T(8,128)}) custom-call(s32[4]{0:T(128)} %pad_add_fusion.refs_0_, bf16[256,640]{1,0:T(8,128)(2,1)} %copy-done.3, bf16[256,640]{1,0:T(8,128)(2,1)} %copy-done.26, ...), custom_call_target="tpu_custom_call" | custom-call | flops 10485760000 | bytes 29360128 | tf_op jit(solution)/shard_map/feed_forward/pallas_call | solution.py:195
  302.2 9.9 %feed_forward_result.1 = (bf16[2,1024,640]{2,1,0:T(8,128)(2,1)}, bf16[2,1024,640]{2,1,0:T(8,128)(2,1)}) custom-call(s32[4]{0:T(128)} %pad_add_fusion.refs_0_, bf16[1024,512]{1,0:T(8,128)(2,1)} %get-tuple-element.153.refs_1_.refs_2_, bf16[160,1280]{1,0:T(8,128)(2,1)} %get-tuple-element.113.refs_11_.refs_37_.refs_2_, ...), custom_call_target="tpu_custom_call" | custom-call | flops 2097152000 | bytes 10485760 | tf_op jit(solution)/shard_map/feed_forward_result/pallas_call | solution.py:195
  316.9 11.7 %feed_forward_grads.3 = (bf16[320,1280]{1,0:T(8,128)(2,1)}, bf16[320,1280]{1,0:T(8,128)(2,1)}, bf16[320,1280]{1,0:T(8,128)(2,1)}, bf16[320,1280]{1,0:T(8,128)(2,1)}) custom-call(s32[4]{0:T(128)} %pad_add_fusion.refs_0_, bf16[1024,896]{1,0:T(8,128)(2,1)} %get-tuple-element.197.refs_1_, bf16[1024,512]{1,0:T(8,128)(2,1)} %get-tuple-element.153.refs_1_.refs_2_, ...), custom_call_target="tpu_custom_call" | custom-call | flops 3145728000 | bytes 18874368 | tf_op jit(solution)/shard_map/feed_forward_grads/pallas_call | solution.py:195
  338.8 11.3 %feed_forward_grads.2 = (bf16[320,1280]{1,0:T(8,128)(2,1)}, bf16[320,1280]{1,0:T(8,128)(2,1)}, bf16[320,1280]{1,0:T(8,128)(2,1)}, bf16[320,1280]{1,0:T(8,128)(2,1)}) custom-call(s32[4]{0:T(128)} %pad_add_fusion.refs_0_, bf16[1024,896]{1,0:T(8,128)(2,1)} %get-tuple-element.197.refs_1_, bf16[1024,512]{1,0:T(8,128)(2,1)} %get-tuple-element.153.refs_1_.refs_2_, ...), custom_call_target="tpu_custom_call" | custom-call | flops 3145728000 | bytes 18874368 | tf_op jit(solution)/shard_map/feed_forward_grads/pallas_call | solution.py:195
  368.5 9.5 %collective-permute-done.84 = bf16[256,640]{1,0:T(8,128)(2,1)S(1)} collective-permute-done((bf16[256,640]{1,0:T(8,128)(2,1)S(1)}, bf16[256,640]{1,0:T(8,128)(2,1)S(1)}, u32[]{:S(2)}, u32[]{:S(2)}) %collective-permute-start.84) | collective-permute-done | bytes 327712 | tf_op jit(solution)/shard_map/ppermute | solution.py:81
  382.9 4.4 collective-permute-start.85
  389.4 6.0 psum.14
  406.3 19.1 %collective-permute-start.129 = (bf16[320,1280]{1,0:T(8,128)(2,1)}, bf16[320,1280]{1,0:T(8,128)(2,1)S(1)}, u32[]{:S(2)}, u32[]{:S(2)}) collective-permute-start(bf16[320,1280]{1,0:T(8,128)(2,1)} %add_convert_fusion), channel_id=1, source_target_pairs={{0,4},{4,0},{8,12},{12,8},{1,5},{5,1},{9,13},{13,9},{2,6},{6,2},{1... | collective-permute-start | bytes 2457608 | tf_op jit(solution)/shard_map/ppermute | solution.py:81
  431.3 4.6 collective-permute-done.129.refs_2_
  436.8 4.4 collective-permute-start.130
  441.2 5.2 output_grads.1
  446.4 23.0 %attention_backward.1 = (bf16[256,1280]{1,0:T(8,128)(2,1)}, bf16[1024,1280]{1,0:T(8,128)(2,1)}, f32[256,768]{1,0:T(8,128)}, f32[256,384]{1,0:T(8,128)}, bf16[256...) custom-call(s32[4]{0:T(128)} %pad_add_fusion.refs_0_, ...), custom_call_target="tpu_custom_call" | custom-call | flops 3355443200 | bytes 25165824 | tf_op jit(solution)/shard_map/attention_backward/pallas_call | solution.py:195
  471.8 6.2 %up_grads.1 = (bf16[128,1280]{1,0:T(8,128)(2,1)}, bf16[128,1280]{1,0:T(8,128)(2,1)}, bf16[128,1280]{1,0:T(8,128)(2,1)}, bf16[128,1280]{1,0:T(8,128)(2,1)}, bf16[...) custom-call(s32[4]{0:T(128)} %pad_add_fusion.refs_0_, ...), custom_call_target="tpu_custom_call" | custom-call | flops 1174405120 | bytes 10485760 | tf_op jit(solution)/shard_map/up_grads/pallas_call | solution.py:195
  482.0 6.0 join_hidden.1
  495.1 5.3 collective-permute-done.99
  501.2 4.5 collective-permute-done.111
  505.9 15.7 %collective-permute-done.121 = bf16[320,640]{1,0:T(8,128)(2,1)S(1)} collective-permute-done((bf16[320,640]{1,0:T(8,128)(2,1)S(1)}, bf16[320,640]{1,0:T(8,128)(2,1)S(1)}, u32[]{:S(2)}, u32[]{:S(2)}) %collective-permute-start.121) | collective-permute-done | bytes 409632 | tf_op jit(solution)/shard_map/ppermute | solution.py:81
  523.1 5.4 collective-permute-done.118
  531.5 6.5 %collective-permute-done.115 = bf16[128,1280]{1,0:T(8,128)(2,1)S(1)} collective-permute-done((bf16[128,1280]{1,0:T(8,128)(2,1)S(1)}, bf16[128,1280]{1,0:T(8,128)(2,1)S(1)}, u32[]{:S(2)}, u32[]{:S(2)}) %collective-permute-start.115) | collective-permute-done | bytes 327712 | tf_op jit(solution)/shard_map/ppermute | solution.py:81
  539.6 5.1 collective-permute-done.101
  550.6 8.1 %collective-permute-done.116 = bf16[128,1280]{1,0:T(8,128)(2,1)S(1)} collective-permute-done((bf16[128,1280]{1,0:T(8,128)(2,1)S(1)}, bf16[128,1280]{1,0:T(8,128)(2,1)S(1)}, u32[]{:S(2)}, u32[]{:S(2)}) %collective-permute-start.116) | collective-permute-done | bytes 327712 | tf_op jit(solution)/shard_map/ppermute | solution.py:81
  561.6 6.1 input_backward.1
  569.0 4.8 collective-permute-done.123
  577.6 20.5 %psum.15 = f32[1280]{0:T(1024)S(1)} all-reduce(f32[1280]{0:T(1024)S(1)} %pad_maximum_fusion.3), channel_id=1, replica_groups=mesh['fsdp'=2,'ctx'=4,'tp'=4] {'fsdp','ctx'}, use_global_device_ids=true, to_apply=%region_4.5 | all-reduce | flops 1280 | bytes 10240 | tf_op jit(solution)/shard_map/psum | solution.py:1394
  605.7 6.0 collective-permute-done.109
  (535 shorter events, 197.9 us)
Async XLA Ops:
  41.7 22.2 %collective-permute-start.64 = (bf16[160,1280]{1,0:T(8,128)(2,1)}, bf16[160,1280]{1,0:T(8,128)(2,1)S(1)}, u32[]{:S(2)}, u32[]{:S(2)}) collective-permute-start(bf16[160,1280]{1,0:T(8,128)(2,1)} %get-tuple-element.124), channel_id=1, source_target_pairs={{0,8},{4,12},{8,0},{12,4},{1,9},{5,13},{9,1},{13,5},{2,10},{6,14},... | collective-permute-start | bytes 1228808 | tf_op jit(solution)/shard_map/ppermute | solution.py:81
  42.0 23.3 %collective-permute-start.65 = (bf16[160,1280]{1,0:T(8,128)(2,1)}, bf16[160,1280]{1,0:T(8,128)(2,1)S(1)}, u32[]{:S(2)}, u32[]{:S(2)}) collective-permute-start(bf16[160,1280]{1,0:T(8,128)(2,1)} %get-tuple-element.125), channel_id=1, source_target_pairs={{0,4},{4,0},{8,12},{12,8},{1,5},{5,1},{9,13},{13,9},{2,6},{6,2},{1... | collective-permute-start | bytes 1228808 | tf_op jit(solution)/shard_map/ppermute | solution.py:81
  56.0 21.2 %collective-permute-start.16 = (bf16[128,1280]{1,0:T(8,128)(2,1)S(1)}, bf16[128,1280]{1,0:T(8,128)(2,1)S(1)}, u32[]{:S(2)}, u32[]{:S(2)}) collective-permute-start(bf16[128,1280]{1,0:T(8,128)(2,1)S(1)} %pad_maximum_fusion.1.refs_9_.refs_2_.refs_11_), channel_id=1, source_target_pairs={{0,8},{4,12},{8,0},{12,4},{1,9},{5,13},{9,1},{13,5},{2,10},{6,14},... | collective-permute-start | bytes 983048 | tf_op jit(solution)/shard_map/ppermute | solution.py:81
  66.1 28.6 %collective-permute-start.23 = (bf16[320,640]{1,0:T(8,128)(2,1)S(1)}, bf16[320,640]{1,0:T(8,128)(2,1)}, u32[]{:S(2)}, u32[]{:S(2)}) collective-permute-start(bf16[320,640]{1,0:T(8,128)(2,1)S(1)} %bitcast.117), channel_id=1, source_target_pairs={{0,8},{4,12},{8,0},{12,4},{1,9},{5,13},{9,1},{13,5},{2,10},{6,14},... | collective-permute-start | bytes 1228808 | tf_op jit(solution)/shard_map/ppermute | solution.py:81
  68.2 27.3 %collective-permute-start.25 = (bf16[320,640]{1,0:T(8,128)(2,1)S(1)}, bf16[320,640]{1,0:T(8,128)(2,1)S(1)}, u32[]{:S(2)}, u32[]{:S(2)}) collective-permute-start(bf16[320,640]{1,0:T(8,128)(2,1)S(1)} %bitcast.118), channel_id=1, source_target_pairs={{0,16},{16,0},{1,17},{17,1},{2,18},{18,2},{3,19},{19,3},{4,20},{20... | collective-permute-start | bytes 1228808 | tf_op jit(solution)/shard_map/ppermute | solution.py:81
  77.2 27.9 %collective-permute-start.68 = (bf16[160,1280]{1,0:T(8,128)(2,1)}, bf16[160,1280]{1,0:T(8,128)(2,1)}, u32[]{:S(2)}, u32[]{:S(2)}) collective-permute-start(bf16[160,1280]{1,0:T(8,128)(2,1)} %get-tuple-element.129.refs_38_.refs_3_), channel_id=1, source_target_pairs={{0,16},{16,0},{1,17},{17,1},{2,18},{18,2},{3,19},{19,3},{4,20},{20... | collective-permute-start | bytes 1228808 | tf_op jit(solution)/shard_map/ppermute | solution.py:81
  78.7 28.2 %collective-permute-start.12 = (f32[128,1152]{1,0:T(8,128)S(1)}, f32[128,1152]{1,0:T(8,128)S(1)}, u32[]{:S(2)}, u32[]{:S(2)}) collective-permute-start(f32[128,1152]{1,0:T(8,128)S(1)} %convert_add_fusion.4.refs_1_), channel_id=1, source_target_pairs={{0,1},{1,0},{2,3},{3,2},{4,5},{5,4},{6,7},{7,6},{8,9},{9,8},{10,11... | collective-permute-start | bytes 1769480 | tf_op jit(solution)/shard_map/ppermute | solution.py:81
  104.7 22.8 %collective-permute-start.69 = (bf16[160,1280]{1,0:T(8,128)(2,1)}, bf16[160,1280]{1,0:T(8,128)(2,1)S(1)}, u32[]{:S(2)}, u32[]{:S(2)}) collective-permute-start(bf16[160,1280]{1,0:T(8,128)(2,1)} %get-tuple-element.134), channel_id=1, source_target_pairs={{0,12},{4,8},{8,4},{12,0},{1,13},{5,9},{9,5},{13,1},{2,14},{6,10},... | collective-permute-start | bytes 1228808 | tf_op jit(solution)/shard_map/ppermute | solution.py:81
  104.7 20.7 %collective-permute-start.24 = (bf16[320,640]{1,0:T(8,128)(2,1)}, bf16[320,640]{1,0:T(8,128)(2,1)}, u32[]{:S(2)}, u32[]{:S(2)}) collective-permute-start(bf16[320,640]{1,0:T(8,128)(2,1)} %collective-permute-done.23.refs_19_.refs_12_.refs_21_), channel_id=1, source_target_pairs={{0,4},{4,0},{8,12},{12,8},{1,5},{5,1},{9,13},{13,9},{2,6},{6,2},{1... | collective-permute-start | bytes 1228808 | tf_op jit(solution)/shard_map/ppermute | solution.py:81
  105.1 21.9 %collective-permute-start.26 = (bf16[320,640]{1,0:T(8,128)(2,1)}, bf16[320,640]{1,0:T(8,128)(2,1)S(1)}, u32[]{:S(2)}, u32[]{:S(2)}) collective-permute-start(bf16[320,640]{1,0:T(8,128)(2,1)} %collective-permute-done.22.refs_18_.refs_11_.refs_20_), channel_id=1, source_target_pairs={{0,16},{16,0},{1,17},{17,1},{2,18},{18,2},{3,19},{19,3},{4,20},{20... | collective-permute-start | bytes 1228808 | tf_op jit(solution)/shard_map/ppermute | solution.py:81
  106.9 22.1 %collective-permute-start.70 = (bf16[160,1280]{1,0:T(8,128)(2,1)}, bf16[160,1280]{1,0:T(8,128)(2,1)S(1)}, u32[]{:S(2)}, u32[]{:S(2)}) collective-permute-start(bf16[160,1280]{1,0:T(8,128)(2,1)} %get-tuple-element.131.refs_39_.refs_4_), channel_id=1, source_target_pairs={{0,16},{16,0},{1,17},{17,1},{2,18},{18,2},{3,19},{19,3},{4,20},{20... | collective-permute-start | bytes 1228808 | tf_op jit(solution)/shard_map/ppermute | solution.py:81
  111.2 21.6 %collective-permute-start.14 = (bf16[256,384]{1,0:T(8,128)(2,1)}, bf16[256,384]{1,0:T(8,128)(2,1)S(1)}, u32[]{:S(2)}, u32[]{:S(2)}) collective-permute-start(bf16[256,384]{1,0:T(8,128)(2,1)} %get-tuple-element.119.refs_5_.refs_7_.refs_4_), channel_id=1, source_target_pairs={{0,8},{4,12},{8,0},{12,4},{1,9},{5,13},{9,1},{13,5},{2,10},{6,14},... | collective-permute-start | bytes 589832 | tf_op jit(solution)/shard_map/ppermute | solution.py:81
  127.0 26.0 %collective-permute-start.28 = (bf16[320,640]{1,0:T(8,128)(2,1)}, bf16[320,640]{1,0:T(8,128)(2,1)S(1)}, u32[]{:S(2)}, u32[]{:S(2)}) collective-permute-start(bf16[320,640]{1,0:T(8,128)(2,1)} %collective-permute-done.24.refs_20_.refs_13_.refs_22_), channel_id=1, source_target_pairs={{0,16},{16,0},{1,17},{17,1},{2,18},{18,2},{3,19},{19,3},{4,20},{20... | collective-permute-start | bytes 1228808 | tf_op jit(solution)/shard_map/ppermute | solution.py:81
  127.5 22.7 %collective-permute-start.21 = (bf16[128,1280]{1,0:T(8,128)(2,1)}, bf16[128,1280]{1,0:T(8,128)(2,1)}, u32[]{:S(2)}, u32[]{:S(2)}) collective-permute-start(bf16[128,1280]{1,0:T(8,128)(2,1)} %collective-permute-done.17.refs_12_.refs_5_.refs_14_), channel_id=1, source_target_pairs={{0,16},{16,0},{1,17},{17,1},{2,18},{18,2},{3,19},{19,3},{4,20},{20... | collective-permute-start | bytes 983048 | tf_op jit(solution)/shard_map/ppermute | solution.py:81
  129.0 25.7 %collective-permute-start.13 = (bf16[256,384]{1,0:T(8,128)(2,1)}, bf16[256,384]{1,0:T(8,128)(2,1)}, u32[]{:S(2)}, u32[]{:S(2)}) collective-permute-start(bf16[256,384]{1,0:T(8,128)(2,1)} %get-tuple-element.119.refs_5_.refs_7_.refs_4_), channel_id=1, source_target_pairs={{0,4},{4,0},{8,12},{12,8},{1,5},{5,1},{9,13},{13,9},{2,6},{6,2},{1... | collective-permute-start | bytes 589832 | tf_op jit(solution)/shard_map/ppermute | solution.py:81
  132.7 24.8 %collective-permute-start.15 = (bf16[256,384]{1,0:T(8,128)(2,1)S(1)}, bf16[256,384]{1,0:T(8,128)(2,1)}, u32[]{:S(2)}, u32[]{:S(2)}) collective-permute-start(bf16[256,384]{1,0:T(8,128)(2,1)S(1)} %collective-permute-done.14.refs_7_.refs_9_.refs_6_), channel_id=1, source_target_pairs={{0,4},{4,0},{8,12},{12,8},{1,5},{5,1},{9,13},{13,9},{2,6},{6,2},{1... | collective-permute-start | bytes 589832 | tf_op jit(solution)/shard_map/ppermute | solution.py:81
  138.1 34.7 %collective-permute-start.62 = (f32[8,640]{1,0:T(8,128)S(1)}, f32[8,640]{1,0:T(8,128)S(1)}, u32[]{:S(2)}, u32[]{:S(2)}) collective-permute-start(f32[8,640]{1,0:T(8,128)S(1)} %broadcast_in_dim.41.refs_33_), channel_id=1, source_target_pairs={{0,2},{1,3},{2,0},{3,1},{4,6},{5,7},{6,4},{7,5},{8,10},{9,11},{10,... | collective-permute-start | bytes 61448 | tf_op jit(solution)/shard_map/ppermute | solution.py:81
  150.2 29.2 %collective-permute-start.47 = (bf16[256,640]{1,0:T(8,128)(2,1)S(1)}, bf16[256,640]{1,0:T(8,128)(2,1)S(1)}, u32[]{:S(2)}, u32[]{:S(2)}) collective-permute-start(bf16[256,640]{1,0:T(8,128)(2,1)S(1)} %fusion.refs_17_.refs_19_), channel_id=1, source_target_pairs={{0,2},{1,3},{2,0},{3,1},{4,6},{5,7},{6,4},{7,5},{8,10},{9,11},{10,... | collective-permute-start | bytes 983048 | tf_op jit(solution)/shard_map/ppermute | solution.py:81
  153.0 26.5 %collective-permute-start.71 = (bf16[160,1280]{1,0:T(8,128)(2,1)}, bf16[160,1280]{1,0:T(8,128)(2,1)S(1)}, u32[]{:S(2)}, u32[]{:S(2)}) collective-permute-start(bf16[160,1280]{1,0:T(8,128)(2,1)} %get-tuple-element.141), channel_id=1, source_target_pairs={{0,8},{4,12},{8,0},{12,4},{1,9},{5,13},{9,1},{13,5},{2,10},{6,14},... | collective-permute-start | bytes 1228808 | tf_op jit(solution)/shard_map/ppermute | solution.py:81
  154.7 24.8 %collective-permute-start.72 = (bf16[160,1280]{1,0:T(8,128)(2,1)}, bf16[160,1280]{1,0:T(8,128)(2,1)S(1)}, u32[]{:S(2)}, u32[]{:S(2)}) collective-permute-start(bf16[160,1280]{1,0:T(8,128)(2,1)} %get-tuple-element.142), channel_id=1, source_target_pairs={{0,4},{4,0},{8,12},{12,8},{1,5},{5,1},{9,13},{13,9},{2,6},{6,2},{1... | collective-permute-start | bytes 1228808 | tf_op jit(solution)/shard_map/ppermute | solution.py:81
  157.5 22.5 %collective-permute-start.73 = (bf16[160,1280]{1,0:T(8,128)(2,1)}, bf16[160,1280]{1,0:T(8,128)(2,1)}, u32[]{:S(2)}, u32[]{:S(2)}) collective-permute-start(bf16[160,1280]{1,0:T(8,128)(2,1)} %get-tuple-element.136.refs_40_.refs_5_), channel_id=1, source_target_pairs={{0,16},{16,0},{1,17},{17,1},{2,18},{18,2},{3,19},{19,3},{4,20},{20... | collective-permute-start | bytes 1228808 | tf_op jit(solution)/shard_map/ppermute | solution.py:81
  181.7 26.6 %collective-permute-start.74 = (bf16[160,1280]{1,0:T(8,128)(2,1)}, bf16[160,1280]{1,0:T(8,128)(2,1)S(1)}, u32[]{:S(2)}, u32[]{:S(2)}) collective-permute-start(bf16[160,1280]{1,0:T(8,128)(2,1)} %get-tuple-element.145.refs_46_.refs_11_), channel_id=1, source_target_pairs={{0,16},{16,0},{1,17},{17,1},{2,18},{18,2},{3,19},{19,3},{4,20},{20... | collective-permute-start | bytes 1228808 | tf_op jit(solution)/shard_map/ppermute | solution.py:81
  328.6 32.3 %collective-permute-start.126 = (bf16[320,1280]{1,0:T(8,128)(2,1)}, bf16[320,1280]{1,0:T(8,128)(2,1)S(1)}, u32[]{:S(2)}, u32[]{:S(2)}) collective-permute-start(bf16[320,1280]{1,0:T(8,128)(2,1)} %get-tuple-element.203), channel_id=1, source_target_pairs={{0,16},{16,0},{1,17},{17,1},{2,18},{18,2},{3,19},{19,3},{4,20},{20... | collective-permute-start | bytes 2457608 | tf_op jit(solution)/shard_map/ppermute | solution.py:81
  330.4 27.0 %collective-permute-start.90 = (bf16[256,640]{1,0:T(8,128)(2,1)}, bf16[256,640]{1,0:T(8,128)(2,1)S(1)}, u32[]{:S(2)}, u32[]{:S(2)}) collective-permute-start(bf16[256,640]{1,0:T(8,128)(2,1)} %get-tuple-element.263), channel_id=1, source_target_pairs={{0,2},{1,3},{2,0},{3,1},{4,6},{5,7},{6,4},{7,5},{8,10},{9,11},{10,... | collective-permute-start | bytes 983048 | tf_op jit(solution)/shard_map/ppermute | solution.py:81
  336.8 22.9 %collective-permute-start.92 = (bf16[256,640]{1,0:T(8,128)(2,1)S(1)}, bf16[256,640]{1,0:T(8,128)(2,1)S(1)}, u32[]{:S(2)}, u32[]{:S(2)}) collective-permute-start(bf16[256,640]{1,0:T(8,128)(2,1)S(1)} %get-tuple-element.266), channel_id=1, source_target_pairs={{0,4},{4,0},{8,12},{12,8},{1,5},{5,1},{9,13},{13,9},{2,6},{6,2},{1... | collective-permute-start | bytes 983048 | tf_op jit(solution)/shard_map/ppermute | solution.py:81
  350.1 31.1 %collective-permute-start.87 = (bf16[256,640]{1,0:T(8,128)(2,1)S(1)}, bf16[256,640]{1,0:T(8,128)(2,1)S(1)}, u32[]{:S(2)}, u32[]{:S(2)}) collective-permute-start(bf16[256,640]{1,0:T(8,128)(2,1)S(1)} %get-tuple-element.261), channel_id=1, source_target_pairs={{0,2},{1,3},{2,0},{3,1},{4,6},{5,7},{6,4},{7,5},{8,10},{9,11},{10,... | collective-permute-start | bytes 983048 | tf_op jit(solution)/shard_map/ppermute | solution.py:81
  357.4 25.4 %collective-permute-start.89 = (bf16[256,640]{1,0:T(8,128)(2,1)S(1)}, bf16[256,640]{1,0:T(8,128)(2,1)S(1)}, u32[]{:S(2)}, u32[]{:S(2)}) collective-permute-start(bf16[256,640]{1,0:T(8,128)(2,1)S(1)} %get-tuple-element.265), channel_id=1, source_target_pairs={{0,4},{4,0},{8,12},{12,8},{1,5},{5,1},{9,13},{13,9},{2,6},{6,2},{1... | collective-permute-start | bytes 983048 | tf_op jit(solution)/shard_map/ppermute | solution.py:81
  361.0 21.9 %collective-permute-start.93 = (bf16[256,640]{1,0:T(8,128)(2,1)S(1)}, bf16[256,640]{1,0:T(8,128)(2,1)S(1)}, u32[]{:S(2)}, u32[]{:S(2)}) collective-permute-start(bf16[256,640]{1,0:T(8,128)(2,1)S(1)} %fusion.7), channel_id=1, source_target_pairs={{0,8},{4,12},{8,0},{12,4},{1,9},{5,13},{9,1},{13,5},{2,10},{6,14},... | collective-permute-start | bytes 983048 | tf_op jit(solution)/shard_map/ppermute | solution.py:81
  367.6 60.9 %collective-permute-start.125 = (bf16[320,1280]{1,0:T(8,128)(2,1)}, bf16[320,1280]{1,0:T(8,128)(2,1)}, u32[]{:S(2)}, u32[]{:S(2)}) collective-permute-start(bf16[320,1280]{1,0:T(8,128)(2,1)} %get-tuple-element.201), channel_id=1, source_target_pairs={{0,16},{16,0},{1,17},{17,1},{2,18},{18,2},{3,19},{19,3},{4,20},{20... | collective-permute-start | bytes 2457608 | tf_op jit(solution)/shard_map/ppermute | solution.py:81
  378.0 26.0 %collective-permute-start.128 = (bf16[320,1280]{1,0:T(8,128)(2,1)}, bf16[320,1280]{1,0:T(8,128)(2,1)}, u32[]{:S(2)}, u32[]{:S(2)}) collective-permute-start(bf16[320,1280]{1,0:T(8,128)(2,1)} %get-tuple-element.205), channel_id=1, source_target_pairs={{0,16},{16,0},{1,17},{17,1},{2,18},{18,2},{3,19},{19,3},{4,20},{20... | collective-permute-start | bytes 2457608 | tf_op jit(solution)/shard_map/ppermute | solution.py:81
  395.7 35.6 %collective-permute-start.127 = (bf16[320,1280]{1,0:T(8,128)(2,1)}, bf16[320,1280]{1,0:T(8,128)(2,1)S(1)}, u32[]{:S(2)}, u32[]{:S(2)}) collective-permute-start(bf16[320,1280]{1,0:T(8,128)(2,1)} %add_convert_fusion.1), channel_id=1, source_target_pairs={{0,12},{4,8},{8,4},{12,0},{1,13},{5,9},{9,5},{13,1},{2,14},{6,10},... | collective-permute-start | bytes 2457608 | tf_op jit(solution)/shard_map/ppermute | solution.py:81
  402.2 26.4 %collective-permute-start.95 = (bf16[256,640]{1,0:T(8,128)(2,1)S(1)}, bf16[256,640]{1,0:T(8,128)(2,1)S(1)}, u32[]{:S(2)}, u32[]{:S(2)}) collective-permute-start(bf16[256,640]{1,0:T(8,128)(2,1)S(1)} %get-tuple-element.256.refs_2_.refs_27_), channel_id=1, source_target_pairs={{0,2},{1,3},{2,0},{3,1},{4,6},{5,7},{6,4},{7,5},{8,10},{9,11},{10,... | collective-permute-start | bytes 983048 | tf_op jit(solution)/shard_map/ppermute | solution.py:81
  406.3 29.6 %collective-permute-start.129 = (bf16[320,1280]{1,0:T(8,128)(2,1)}, bf16[320,1280]{1,0:T(8,128)(2,1)S(1)}, u32[]{:S(2)}, u32[]{:S(2)}) collective-permute-start(bf16[320,1280]{1,0:T(8,128)(2,1)} %add_convert_fusion), channel_id=1, source_target_pairs={{0,4},{4,0},{8,12},{12,8},{1,5},{5,1},{9,13},{13,9},{2,6},{6,2},{1... | collective-permute-start | bytes 2457608 | tf_op jit(solution)/shard_map/ppermute | solution.py:81
  426.7 52.0 %collective-permute-start.124 = (bf16[320,1280]{1,0:T(8,128)(2,1)}, bf16[320,1280]{1,0:T(8,128)(2,1)}, u32[]{:S(2)}, u32[]{:S(2)}) collective-permute-start(bf16[320,1280]{1,0:T(8,128)(2,1)} %get-tuple-element.199), channel_id=1, source_target_pairs={{0,16},{16,0},{1,17},{17,1},{2,18},{18,2},{3,19},{19,3},{4,20},{20... | collective-permute-start | bytes 2457608 | tf_op jit(solution)/shard_map/ppermute | solution.py:81
  436.8 44.3 %collective-permute-start.130 = (bf16[320,1280]{1,0:T(8,128)(2,1)}, bf16[320,1280]{1,0:T(8,128)(2,1)S(1)}, u32[]{:S(2)}, u32[]{:S(2)}) collective-permute-start(bf16[320,1280]{1,0:T(8,128)(2,1)} %get-tuple-element.207), channel_id=1, source_target_pairs={{0,8},{4,12},{8,0},{12,4},{1,9},{5,13},{9,1},{13,5},{2,10},{6,14},... | collective-permute-start | bytes 2457608 | tf_op jit(solution)/shard_map/ppermute | solution.py:81
  488.0 43.4 %collective-permute-start.113 = (bf16[128,1280]{1,0:T(8,128)(2,1)S(1)}, bf16[128,1280]{1,0:T(8,128)(2,1)S(1)}, u32[]{:S(2)}, u32[]{:S(2)}) collective-permute-start(bf16[128,1280]{1,0:T(8,128)(2,1)S(1)} %copy-done.96), channel_id=1, source_target_pairs={{0,16},{16,0},{1,17},{17,1},{2,18},{18,2},{3,19},{19,3},{4,20},{20... | collective-permute-start | bytes 983048 | tf_op jit(solution)/shard_map/ppermute | solution.py:81
  490.1 57.7 %collective-permute-start.110 = (bf16[128,1280]{1,0:T(8,128)(2,1)S(1)}, bf16[128,1280]{1,0:T(8,128)(2,1)S(1)}, u32[]{:S(2)}, u32[]{:S(2)}) collective-permute-start(bf16[128,1280]{1,0:T(8,128)(2,1)S(1)} %copy-done.95), channel_id=1, source_target_pairs={{0,16},{16,0},{1,17},{17,1},{2,18},{18,2},{3,19},{19,3},{4,20},{20... | collective-permute-start | bytes 983048 | tf_op jit(solution)/shard_map/ppermute | solution.py:81
  494.2 27.3 %collective-permute-start.121 = (bf16[320,640]{1,0:T(8,128)(2,1)S(1)}, bf16[320,640]{1,0:T(8,128)(2,1)S(1)}, u32[]{:S(2)}, u32[]{:S(2)}) collective-permute-start(bf16[320,640]{1,0:T(8,128)(2,1)S(1)} %copy-done.93), channel_id=1, source_target_pairs={{0,16},{16,0},{1,17},{17,1},{2,18},{18,2},{3,19},{19,3},{4,20},{20... | collective-permute-start | bytes 1228808 | tf_op jit(solution)/shard_map/ppermute | solution.py:81
  500.4 28.1 %collective-permute-start.118 = (bf16[320,640]{1,0:T(8,128)(2,1)S(1)}, bf16[320,640]{1,0:T(8,128)(2,1)S(1)}, u32[]{:S(2)}, u32[]{:S(2)}) collective-permute-start(bf16[320,640]{1,0:T(8,128)(2,1)S(1)} %copy-done.92), channel_id=1, source_target_pairs={{0,16},{16,0},{1,17},{17,1},{2,18},{18,2},{3,19},{19,3},{4,20},{20... | collective-permute-start | bytes 1228808 | tf_op jit(solution)/shard_map/ppermute | solution.py:81
  505.8 23.6 %collective-permute-start.100 = (f32[128,1152]{1,0:T(8,128)S(1)}, f32[128,1152]{1,0:T(8,128)S(1)}, u32[]{:S(2)}, u32[]{:S(2)}) collective-permute-start(f32[128,1152]{1,0:T(8,128)S(1)} %dynamic-slice_bitcast_fusion), channel_id=1, source_target_pairs={{0,1},{1,0},{2,3},{3,2},{4,5},{5,4},{6,7},{7,6},{8,9},{9,8},{10,11... | collective-permute-start | bytes 1769480 | tf_op jit(solution)/shard_map/ppermute | solution.py:81
  521.6 24.3 %collective-permute-start.120 = (bf16[320,640]{1,0:T(8,128)(2,1)S(1)}, bf16[320,640]{1,0:T(8,128)(2,1)S(1)}, u32[]{:S(2)}, u32[]{:S(2)}) collective-permute-start(bf16[320,640]{1,0:T(8,128)(2,1)S(1)} %copy-done.91), channel_id=1, source_target_pairs={{0,16},{16,0},{1,17},{17,1},{2,18},{18,2},{3,19},{19,3},{4,20},{20... | collective-permute-start | bytes 1228808 | tf_op jit(solution)/shard_map/ppermute | solution.py:81
  545.8 22.0 %collective-permute-start.117 = (bf16[320,640]{1,0:T(8,128)(2,1)}, bf16[320,640]{1,0:T(8,128)(2,1)S(1)}, u32[]{:S(2)}, u32[]{:S(2)}) collective-permute-start(bf16[320,640]{1,0:T(8,128)(2,1)} %get-tuple-element.190), channel_id=1, source_target_pairs={{0,16},{16,0},{1,17},{17,1},{2,18},{18,2},{3,19},{19,3},{4,20},{20... | collective-permute-start | bytes 1228808 | tf_op jit(solution)/shard_map/ppermute | solution.py:81
  547.9 21.1 %collective-permute-start.119 = (bf16[320,640]{1,0:T(8,128)(2,1)}, bf16[320,640]{1,0:T(8,128)(2,1)S(1)}, u32[]{:S(2)}, u32[]{:S(2)}) collective-permute-start(bf16[320,640]{1,0:T(8,128)(2,1)} %add_convert_fusion.7), channel_id=1, source_target_pairs={{0,4},{4,0},{8,12},{12,8},{1,5},{5,1},{9,13},{13,9},{2,6},{6,2},{1... | collective-permute-start | bytes 1228808 | tf_op jit(solution)/shard_map/ppermute | solution.py:81
  549.9 23.9 %collective-permute-start.123 = (bf16[320,640]{1,0:T(8,128)(2,1)}, bf16[320,640]{1,0:T(8,128)(2,1)S(1)}, u32[]{:S(2)}, u32[]{:S(2)}) collective-permute-start(bf16[320,640]{1,0:T(8,128)(2,1)} %add_convert_fusion.4), channel_id=1, source_target_pairs={{0,8},{4,12},{8,0},{12,4},{1,9},{5,13},{9,1},{13,5},{2,10},{6,14},... | collective-permute-start | bytes 1228808 | tf_op jit(solution)/shard_map/ppermute | solution.py:81
  567.8 30.2 %collective-permute-start.107 = (bf16[144,640]{1,0:T(8,128)(2,1)}, bf16[144,640]{1,0:T(8,128)(2,1)S(1)}, u32[]{:S(2)}, u32[]{:S(2)}) collective-permute-start(bf16[144,640]{1,0:T(8,128)(2,1)} %get-tuple-element.179), channel_id=1, source_target_pairs={{0,16},{16,0},{1,17},{17,1},{2,18},{18,2},{3,19},{19,3},{4,20},{20... | collective-permute-start | bytes 552968 | tf_op jit(solution)/shard_map/ppermute | solution.py:81
  574.9 25.4 %collective-permute-start.106 = (bf16[144,640]{1,0:T(8,128)(2,1)S(1)}, bf16[144,640]{1,0:T(8,128)(2,1)S(1)}, u32[]{:S(2)}, u32[]{:S(2)}) collective-permute-start(bf16[144,640]{1,0:T(8,128)(2,1)S(1)} %copy-done.101), channel_id=1, source_target_pairs={{0,16},{16,0},{1,17},{17,1},{2,18},{18,2},{3,19},{19,3},{4,20},{20... | collective-permute-start | bytes 552968 | tf_op jit(solution)/shard_map/ppermute | solution.py:81
  575.5 22.7 %collective-permute-start.104 = (bf16[144,640]{1,0:T(8,128)(2,1)S(1)}, bf16[144,640]{1,0:T(8,128)(2,1)S(1)}, u32[]{:S(2)}, u32[]{:S(2)}) collective-permute-start(bf16[144,640]{1,0:T(8,128)(2,1)S(1)} %copy-done.102), channel_id=1, source_target_pairs={{0,16},{16,0},{1,17},{17,1},{2,18},{18,2},{3,19},{19,3},{4,20},{20... | collective-permute-start | bytes 552968 | tf_op jit(solution)/shard_map/ppermute | solution.py:81
  576.9 27.6 %collective-permute-start.103 = (bf16[144,640]{1,0:T(8,128)(2,1)S(1)}, bf16[144,640]{1,0:T(8,128)(2,1)S(1)}, u32[]{:S(2)}, u32[]{:S(2)}) collective-permute-start(bf16[144,640]{1,0:T(8,128)(2,1)S(1)} %copy-done.100), channel_id=1, source_target_pairs={{0,16},{16,0},{1,17},{17,1},{2,18},{18,2},{3,19},{19,3},{4,20},{20... | collective-permute-start | bytes 552968 | tf_op jit(solution)/shard_map/ppermute | solution.py:81
  (189 other events, 2909.0 us)
